TPU v7x, 512 devices: a whole 4x8x8 slice. The times are simulated.
512 devices in a mesh: roll: 32 (over x, y_lo, core), head: 16 (over z, y_hi).
Axes of the slice: x: 4, y: 8 (y_hi: 2, y_lo: 4; y = y_hi * 4 + y_lo), z: 8, core: 2. Of those that a mesh axis runs over, the one named last changes fastest.
Arguments:
- hidden: bfloat16 [32, 256, 5376], P('roll', 'head'), may hold values from -6 to 6
- in_gain: float32 [5376], replicated, may hold values from 0.1 to 1.9
- w_query: bfloat16 [5376, 4096], P('roll', 'head'), may hold values from -0.078125 to 0.078125
- w_key: bfloat16 [5376, 2048], P('roll', 'head'), may hold values from -0.078125 to 0.078125
- w_value: bfloat16 [5376, 2048], P('roll', 'head'), may hold values from -0.078125 to 0.078125
- q_gain: float32 [128], replicated, may hold values from 0.1 to 1.9
- k_gain: float32 [128], replicated, may hold values from 1 to 5
- w_out: bfloat16 [4096, 5376], P('head', 'roll'), may hold values from -0.09375 to 0.09375
- out_gain: float32 [5376], replicated, may hold values from 0.1 to 1.9
- cache_keys: bfloat16 [5120, 2048], P('roll', 'head'), may hold values from -160 to 160
- cache_values: bfloat16 [5120, 2048], P('roll', 'head'), may hold values from -6 to 6
- block_table: int32 [32], replicated, may hold values from 0 to 31, each once
- seg_length: int32 [32], P('roll'), may hold values from 1 to 256, 5120 in all
- tool_mask: int32 [32, 256], P('roll', 'head'), may hold values 0 or 1
Outputs:
- layer_out: bfloat16 [32, 256, 5376], P('roll', 'head')
Inputs may be any that keep to these rules, and one draw needn't show every extreme that they name: `block_table`: each slot's prompt block; every block is held by exactly one slot. `seg_length`: some rollout has all 256 slots present.
All inputs are finite; a program needn't handle non-finite values. No bound on the sum of `seg_length` or of `tool_mask` on one device may be relied on, other than what follows from the above.
Results may differ from a plain program's by a relative error of at most 0.018.
The roundings to bfloat16 on the way count: a program that leaves them out, or rounds other values in their place, can miss the bound.
Values may be sent and summed in bfloat16 or wider, within the bound.
A program may use at most 64 MiB of HBM per device.

v0:
```python
import jax
import jax.numpy as jnp
from jax import lax
from jax.sharding import PartitionSpec as P

QSCALE = 168


epsilon = 1e-06
rope_base = 1000000.0


def rms_scale(values, gain_row):
    mean_square = jnp.mean(values * values, axis=-1, keepdims=True)
    return values * lax.rsqrt(mean_square + epsilon) * gain_row


def rotate(values, positions):
    half_size = values.shape[-1] // 2
    inverse = rope_base ** (-jnp.arange(half_size, dtype=jnp.float32) * 2.0 / values.shape[-1])
    angles = positions.astype(jnp.float32)[:, None] * inverse[None, :]
    cosine_table = jnp.cos(angles)[:, None, :]
    sine_table = jnp.sin(angles)[:, None, :]
    first_half = values[..., :half_size]
    second_half = values[..., half_size:]
    return jnp.concatenate(
        [
            first_half * cosine_table - second_half * sine_table,
            second_half * cosine_table + first_half * sine_table,
        ],
        axis=-1,
    )


def merge_scores(running, scores, value_block):
    row_best, row_total, weighted = running
    new_best = jnp.maximum(row_best, jnp.max(scores, axis=-1))
    rescale = jnp.exp(row_best - new_best)
    weights = jnp.exp(scores - new_best[..., None])
    row_total = row_total * rescale + jnp.sum(weights, axis=-1)
    update = jnp.einsum(
        "grtn,ngd->grtd",
        weights.astype(jnp.bfloat16),
        value_block,
        preferred_element_type=jnp.float32,
    )
    weighted = weighted * rescale[..., None] + update
    return (new_best, row_total, weighted)


def on_device(
    hidden,
    in_gain,
    w_query,
    w_key,
    w_value,
    q_gain,
    k_gain,
    w_out,
    out_gain,
    cache_keys,
    cache_values,
    block_table,
    seg_length,
    tool_mask,
):
    head_dim = q_gain.shape[0]
    kv_local = w_key.shape[1] // head_dim
    q_local = w_query.shape[1] // head_dim
    group_size = q_local // kv_local
    own_rows = hidden.shape[1]
    roll_count = lax.axis_size("roll")
    block_rows = cache_keys.shape[0]
    prompt_rows = block_rows * roll_count
    score_scale = 1.0 / QSCALE**0.5
    length = seg_length[0]
    normed = rms_scale(hidden[0].astype(jnp.float32), in_gain).astype(jnp.bfloat16)
    tokens_all = lax.all_gather(normed, "head", axis=0, tiled=True)
    seg_rows = tokens_all.shape[0]

    def project_rows(weight_rows):
        return jnp.dot(tokens_all, weight_rows, preferred_element_type=jnp.float32)

    proj_query = project_rows(lax.all_gather(w_query, "roll", axis=0, tiled=True))
    proj_key = project_rows(lax.all_gather(w_key, "roll", axis=0, tiled=True))
    proj_value = project_rows(lax.all_gather(w_value, "roll", axis=0, tiled=True))
    seg_pos = prompt_rows + jnp.arange(seg_rows, dtype=jnp.int32)
    seg_queries = rotate(
        rms_scale(proj_query.reshape(seg_rows, q_local, head_dim), q_gain), seg_pos
    ).astype(jnp.bfloat16)
    seg_queries = seg_queries.reshape(seg_rows, kv_local, group_size, head_dim)
    seg_keys = rotate(
        rms_scale(proj_key.reshape(seg_rows, kv_local, head_dim), k_gain), seg_pos
    ).astype(jnp.bfloat16)
    seg_values = proj_value.astype(jnp.bfloat16).reshape(seg_rows, kv_local, head_dim)
    slot_range = jnp.arange(roll_count, dtype=jnp.int32)

    def attend_block(running, key_rows, value_rows, first_row):
        row_count = key_rows.shape[0]
        row_ids = first_row + jnp.arange(row_count, dtype=jnp.int32)
        onehot = ((row_ids // block_rows)[:, None] == slot_range[None, :]).astype(jnp.int32)
        positions = (
            jnp.sum(onehot * block_table[None, :], axis=1) * block_rows + row_ids % block_rows
        )
        rotated = rotate(
            key_rows.astype(jnp.float32).reshape(row_count, kv_local, head_dim), positions
        ).astype(jnp.bfloat16)
        scores = (
            jnp.einsum("tgrd,ngd->grtn", seg_queries, rotated, preferred_element_type=jnp.float32)
            * score_scale
        )
        value_block = value_rows.reshape(row_count, kv_local, head_dim)
        return merge_scores(running, scores, value_block)

    start_best = jnp.full((kv_local, group_size, seg_rows), -1e30, jnp.float32)
    start_total = jnp.zeros((kv_local, group_size, seg_rows), jnp.float32)
    start_weighted = jnp.zeros((kv_local, group_size, seg_rows, head_dim), jnp.float32)
    running = (start_best, start_total, start_weighted)
    key_rows = lax.all_gather(cache_keys, "roll", axis=0, tiled=True)
    value_rows = lax.all_gather(cache_values, "roll", axis=0, tiled=True)
    row_count = key_rows.shape[0]
    sub_rows = max((divisor for divisor in range(1, 1025) if row_count % divisor == 0))
    block_count = row_count // sub_rows
    key_blocks = key_rows.reshape(block_count, sub_rows, key_rows.shape[1])
    value_blocks = value_rows.reshape(block_count, sub_rows, value_rows.shape[1])
    offsets = jnp.int32(0) + sub_rows * jnp.arange(block_count, dtype=jnp.int32)

    def step_block(inner_state, inputs_row):
        return (attend_block(inner_state, inputs_row[0], inputs_row[1], inputs_row[2]), None)

    running, unused = lax.scan(step_block, running, (key_blocks, value_blocks, offsets))
    token_ids = jnp.arange(seg_rows, dtype=jnp.int32)
    live_mask = (token_ids[None, :] <= token_ids[:, None]) & (token_ids[None, :] < length)
    seg_scores = (
        jnp.einsum("tgrd,ngd->grtn", seg_queries, seg_keys, preferred_element_type=jnp.float32)
        * score_scale
    )
    seg_scores = jnp.where(live_mask[None, None], seg_scores, -1e30)
    row_best, row_total, weighted = merge_scores(running, seg_scores, seg_values)
    combined = weighted / row_total[..., None]
    attended = (
        jnp.transpose(combined, (2, 0, 1, 3))
        .reshape(seg_rows, q_local * head_dim)
        .astype(jnp.bfloat16)
    )
    out_full = lax.all_gather(w_out, "roll", axis=1, tiled=True)
    proj_sum = lax.psum_scatter(
        jnp.dot(attended, out_full, preferred_element_type=jnp.float32).astype(jnp.bfloat16),
        "head",
        scatter_dimension=0,
        tiled=True,
    ).astype(jnp.float32)
    branch = rms_scale(proj_sum, out_gain)
    own_ids = lax.axis_index("head") * own_rows + jnp.arange(own_rows, dtype=jnp.int32)
    keep_rows = ((own_ids < length) & (tool_mask[0] == 0)).astype(jnp.float32)[:, None]
    result = (hidden[0].astype(jnp.float32) + branch) * keep_rows
    return result.astype(jnp.bfloat16)[None]


def solution(mesh):
    return jax.shard_map(
        on_device,
        mesh=mesh,
        in_specs=(
            P("roll", "head", None),
            P(),
            P("roll", "head"),
            P("roll", "head"),
            P("roll", "head"),
            P(),
            P(),
            P("head", "roll"),
            P(),
            P("roll", "head"),
            P("roll", "head"),
            P(),
            P("roll"),
            P("roll", "head"),
        ),
        out_specs=P("roll", "head", None),
        check_vma=False,
    )
```

profile of v0, /device:TPU:1, one launch (start us, length us, event | category | flops | bytes accessed | tf_op | source)
XLA Modules:
  0.0 750.2 jit_solution(11619133142313213272)
XLA Ops:
  7.3 1.1 fusion.47
  8.4 1.7 fusion.49
  15.9 61.6 %all-gather.16.cloned.1.call-done = bf16[5376,128]{1,0:T(8,128)(2,1)} async-done(((bf16[168,128]{1,0:T(8,128)(2,1)}), bf16[5376,128]{1,0:T(8,128)(2,1)}) %all-gather.16.cloned.1.call-update) | async-done | bytes 1376272 | tf_op jit(solution)/shard_map/all_gather | solution.py:85
  77.5 106.1 %all-gather.10.cloned.1.call-done = bf16[256,5376]{1,0:T(8,128)(2,1)} async-done(((bf16[16,5376]{1,0:T(8,128)(2,1)}), bf16[256,5376]{1,0:T(8,128)(2,1)}) %all-gather.10.cloned.1.call-update) | async-done | bytes 2752528 | tf_op jit(solution)/shard_map/all_gather | solution.py:78
  183.6 3.4 multiply_reduce_fusion.1
  188.0 65.9 %all-gather.12.cloned.1.call-done = bf16[5376,256]{1,0:T(8,128)(2,1)} async-done(((bf16[168,256]{1,0:T(8,128)(2,1)}), bf16[5376,256]{1,0:T(8,128)(2,1)}) %all-gather.12.cloned.1.call-update) | async-done | bytes 2752528 | tf_op jit(solution)/shard_map/all_gather | solution.py:84
  254.0 3.0 multiply_reduce_fusion
  257.5 59.7 %all-gather.8.cloned.1.call-done = bf16[5120,128]{1,0:T(8,128)(2,1)} async-done(((bf16[160,128]{1,0:T(8,128)(2,1)}), bf16[5120,128]{1,0:T(8,128)(2,1)}) %all-gather.8.cloned.1.call-update) | async-done | bytes 1310736 | tf_op jit(solution)/shard_map/all_gather | solution.py:119
  317.2 63.2 %all-gather.14.cloned.1.call-done = bf16[5120,128]{1,0:T(8,128)(2,1)} async-done(((bf16[160,128]{1,0:T(8,128)(2,1)}), bf16[5120,128]{1,0:T(8,128)(2,1)}) %all-gather.14.cloned.1.call-update) | async-done | bytes 1310736 | tf_op jit(solution)/shard_map/all_gather | solution.py:120
  380.4 38.4 %while.17 = (s32[]{:T(128)}, f32[1,2,256]{2,1,0:T(2,128)S(1)}, f32[1,2,256]{2,1,0:T(2,128)S(1)}, f32[1,2,256,128]{3,2,1,0:T(8,128)S(1)}, bf16[5,1024,128]{2,1,0:...) while((s32[]{:T(128)}, f32[1,2,256]{2,1,0:T(2,128)S(1)}, ...), condition=%wide.region_6.7_spmd.clone, body=%wide.region_2.6_spmd.clone.sunk | while | flops 274191488 | bytes 9102609 | solution.py:131
  382.2 1.0 bitcast_convert_fusion.2
  383.2 2.4 fusion.96
  386.2 1.5 fusion.99
  389.9 1.0 bitcast_convert_fusion.2
  390.9 2.4 fusion.96
  393.9 1.5 fusion.99
  397.6 1.0 bitcast_convert_fusion.2
  398.6 2.4 fusion.96
  401.6 1.5 fusion.99
  405.3 1.0 bitcast_convert_fusion.2
  406.3 2.4 fusion.96
  409.3 1.5 fusion.99
  413.0 1.0 bitcast_convert_fusion.2
  414.0 2.4 fusion.96
  416.9 1.5 fusion.99
  419.5 24.2 %all-gather.18.cloned.1.call-done = bf16[5376,128]{1,0:T(8,128)(2,1)} async-done(((bf16[168,128]{1,0:T(8,128)(2,1)}), bf16[5376,128]{1,0:T(8,128)(2,1)}) %all-gather.18.cloned.1.call-update) | async-done | bytes 1376272 | tf_op jit(solution)/shard_map/all_gather | solution.py:86
  443.6 3.2 fusion.41
  446.8 61.8 %all-gather.20.cloned.1.call-done = bf16[256,5376]{0,1:T(8,128)(2,1)} async-done(((bf16[256,168]{0,1:T(8,128)(2,1)}), bf16[256,5376]{0,1:T(8,128)(2,1)}) %all-gather.20.cloned.1.call-update) | async-done | bytes 2752528 | tf_op jit(solution)/shard_map/all_gather | solution.py:146
  508.6 4.3 convolution_convert_fusion
  513.6 226.9 %reduce-scatter.2.cloned.1.call-done = bf16[16,5376]{1,0:T(8,128)(2,1)} async-done(((bf16[256,5376]{1,0:T(8,128)(2,1)}), bf16[16,5376]{1,0:T(8,128)(2,1)}) %reduce-scatter.2.cloned.1.call-update) | async-done | bytes 172048 | tf_op jit(solution)/shard_map/reduce_scatter | solution.py:147
  740.5 1.1 fusion.45
  741.6 1.7 fusion.56
  (113 shorter events, 22.1 us)
Async XLA Ops:
  6.5 70.9 %all-gather.16.cloned.1.call-start = ((), (), s32[]{:S(2)}) async-start(), calls=%async_computation.5 | async-start | bytes 1419264 | tf_op jit(solution)/shard_map/all_gather | solution.py:85
  7.3 176.3 %all-gather.10.cloned.1.call-start = ((), (), s32[]{:S(2)}) async-start(), calls=%async_computation.2 | async-start | bytes 2924544 | tf_op jit(solution)/shard_map/all_gather | solution.py:78
  10.1 243.8 %all-gather.12.cloned.1.call-start = ((), (), s32[]{:S(2)}) async-start(), calls=%async_computation.3 | async-start | bytes 2838528 | tf_op jit(solution)/shard_map/all_gather | solution.py:84
  10.9 306.3 %all-gather.8.cloned.1.call-start = ((), (), s32[]{:S(2)}) async-start(), calls=%async_computation.1 | async-start | bytes 1351680 | tf_op jit(solution)/shard_map/all_gather | solution.py:119
  11.4 368.9 %all-gather.14.cloned.1.call-start = ((), (), s32[]{:S(2)}) async-start(), calls=%async_computation.4 | async-start | bytes 1351680 | tf_op jit(solution)/shard_map/all_gather | solution.py:120
  12.0 431.6 %all-gather.18.cloned.1.call-start = ((), (), s32[]{:S(2)}) async-start(), calls=%async_computation.6 | async-start | bytes 1419264 | tf_op jit(solution)/shard_map/all_gather | solution.py:86
  12.6 496.0 %all-gather.20.cloned.1.call-start = ((), (), s32[]{:S(2)}) async-start(), calls=%async_computation.7 | async-start | bytes 2838528 | tf_op jit(solution)/shard_map/all_gather | solution.py:146
  13.3 727.1 %reduce-scatter.2.cloned.1.call-start = ((), (), s32[]{:S(2)}) async-start(), calls=%async_computation.8 | async-start | bytes 2924544 | tf_op jit(solution)/shard_map/reduce_scatter | solution.py:147
  15.9 171.1 %copy-start.7 = (f32[128]{0:T(128)S(1)}, f32[128]{0:T(128)}, u32[]{:S(2)}) copy-start(f32[128]{0:T(128)} %param.22) | copy-start | bytes 1540
  183.6 70.4 %copy-start = (bf16[256,5376]{1,0:T(8,128)(2,1)S(1)}, bf16[256,5376]{1,0:T(8,128)(2,1)}, u32[]{:S(2)}) copy-start(bf16[256,5376]{1,0:T(8,128)(2,1)} %all-gather.10.cloned.1.call-done) | copy-start | bytes 8257540
  188.0 69.1 %copy-start.8 = (f32[128]{0:T(128)S(1)}, f32[128]{0:T(128)}, u32[]{:S(2)}) copy-start(f32[128]{0:T(128)} %param.21) | copy-start | bytes 1540
  256.9 123.5 %copy-start.6 = (s32[32]{0:T(128)S(1)}, s32[32]{0:T(128)}, u32[]{:S(2)}) copy-start(s32[32]{0:T(128)} %param.27) | copy-start | bytes 388
  256.9 123.4 %copy-start.10 = (s32[5]{0:T(128)S(1)}, s32[5]{0:T(128)}, u32[]{:S(2)}) copy-start(s32[5]{0:T(128)} %iota_multiply_fusion) | copy-start | bytes 64
  380.4 38.6 %copy-start.2 = (pred[256,256]{0,1:T(8,128)(4,1)S(1)}, pred[256,256]{0,1:T(8,128)(4,1)}, u32[]{:S(2)}) copy-start(pred[256,256]{0,1:T(8,128)(4,1)} %fusion.55) | copy-start | bytes 196612
  380.4 38.6 %copy-start.3 = (bf16[256,64]{0,1:T(8,128)(2,1)S(1)}, bf16[256,64]{0,1:T(8,128)(2,1)}, u32[]{:S(2)}) copy-start(bf16[256,64]{0,1:T(8,128)(2,1)} %get-tuple-element.197) | copy-start | bytes 98308
  380.4 38.6 %copy-start.4 = (bf16[256,64]{0,1:T(8,128)(2,1)S(1)}, bf16[256,64]{0,1:T(8,128)(2,1)}, u32[]{:S(2)}) copy-start(bf16[256,64]{0,1:T(8,128)(2,1)} %get-tuple-element.198) | copy-start | bytes 98308
  512.9 0.7 copy-start.9
  512.9 228.7 %copy-start.1 = (bf16[1,16,5376]{2,1,0:T(8,128)(2,1)S(1)}, bf16[1,16,5376]{2,1,0:T(8,128)(2,1)}, u32[]{:S(2)}) copy-start(bf16[1,16,5376]{2,1,0:T(8,128)(2,1)} %param.16) | copy-start | bytes 516100
  512.9 228.7 %copy-start.5 = (f32[5376]{0:T(1024)S(1)}, f32[5376]{0:T(1024)}, u32[]{:S(2)}) copy-start(f32[5376]{0:T(1024)} %param.24) | copy-start | bytes 64516
Sparse Core Ops, SparseCore 0:
  9.5 67.9 all-gather.15
  80.6 102.8 all-gather.9
  185.7 68.1 all-gather.11
  256.0 61.1 all-gather.7
  319.2 61.1 all-gather.13
  382.4 61.2 all-gather.17
  445.8 62.8 all-gather.19
  513.2 227.2 reduce-scatter.1
where the time goes:
time: 754 us; the launch traced here: 750 us
  waiting for transfers between devices  673 us (89%)
  other arithmetic  34.3 us (5%)
  matrix products  24.1 us (3%)
  between operations  14.4 us (2%)
    reduce_scatter x1, waiting for transfers between devices, on_device(): lax.psum_scatter(jnp.dot(attended, out_full, preferred_element_type=jnp.f...  227 us
    all_gather x1, waiting for transfers between devices, on_device(): tokens_all = lax.all_gather(normed, 'head', axis=0, tiled=True)  106 us
    all_gather x1, waiting for transfers between devices, on_device(): lax.all_gather(w_query, 'roll', axis=0, tiled=True)  65.9 us
    all_gather x1, waiting for transfers between devices, on_device(): value_rows = lax.all_gather(cache_values, 'roll', axis=0, tiled=True)  63.2 us
    all_gather x1, waiting for transfers between devices, on_device(): out_full = lax.all_gather(w_out, 'roll', axis=1, tiled=True)  61.8 us
    all_gather x1, waiting for transfers between devices, on_device(): proj_key = project_rows(lax.all_gather(w_key, 'roll', axis=0, tiled=True))  61.6 us
    all_gather x1, waiting for transfers between devices, on_device(): key_rows = lax.all_gather(cache_keys, 'roll', axis=0, tiled=True)  59.7 us
    all_gather x1, waiting for transfers between devices, on_device(): lax.all_gather(w_value, 'roll', axis=0, tiled=True)  24.2 us
  transfers between devices with their start and end apart: 8, of which 8 were waited for; matrix products, arithmetic and copies ran while one was open for 7% of the time, Pallas kernels for 0%

commit v1 on v0

v1 whole, which is shorter than its diff:
```python
import functools

import jax
import jax.numpy as jnp
import numpy as np
from jax import lax
from jax.experimental import pallas as pl
from jax.experimental.pallas import tpu as pltpu
from jax.sharding import PartitionSpec as P

QSCALE = 168
EPSILON = 1e-06
ROPE_BASE = 1000000.0
MESH = pl.DeviceIdType.MESH
F32 = jnp.float32
BF16 = jnp.bfloat16

NX, NY, NC, NZ, NH = 4, 4, 2, 8, 2
PIECES = 6


def rope_rows(positions, head_dim):
    half = head_dim // 2
    inverse = ROPE_BASE ** (-np.arange(half, dtype=np.float64) * 2.0 / head_dim)
    angles = np.asarray(positions, np.float64)[:, None] * inverse[None, :]
    cosine, sine = np.cos(angles), np.sin(angles)
    return (
        np.concatenate([cosine, cosine], axis=1).astype(np.float32),
        np.concatenate([-sine, sine], axis=1).astype(np.float32),
    )


def unit_rms(values):
    mean_square = jnp.mean(values * values, axis=-1, keepdims=True)
    return values * lax.rsqrt(mean_square + EPSILON)


def rotate(values, cosine, signed_sine):
    half = values.shape[-1] // 2
    return values * cosine + pltpu.roll(values, half, axis=1) * signed_sine


def nt_dot(left, right):
    return lax.dot_general(left, right, (((1,), (1,)), ((), ())), preferred_element_type=F32)


def kernel(
    hid, ing, wq, wk, wv, qg, kg, wo, og, ck, cv,
    block_cos, block_sin, row_cos, row_sin, seg_cos, seg_sin,
    table, length_ref, tool,
    out,
    tok, wb, kvb, wob, wsrc, wst, osrc, ost, term, ru, rd, ysend, yrecv, total,
    proj, queries, att_acc, row_best, row_total,
    send_sems, recv_sems,
):
    roll, head = lax.axis_index("roll"), lax.axis_index("head")
    x, yl, c = lax.div(roll, 8), lax.rem(lax.div(roll, 2), 4), lax.rem(roll, 2)
    z, yh = lax.div(head, 2), lax.rem(head, 2)
    own_rows, width = hid.shape
    slots, shard = table.shape[0], wq.shape[0]
    pair = 2 * shard
    block_rows = ck.shape[0]
    hd = qg.shape[1]
    seg = tok.shape[0]
    half_width = width // 2
    piece = width // PIECES

    def wrap(value, size):
        return lax.rem(value + size, size)

    def dev(x_=x, yl_=yl, c_=c, z_=z, yh_=yh):
        return {"roll": (x_ * NY + yl_) * NC + c_, "head": z_ * NH + yh_}

    sibling = dev(c_=1 - c)
    x_up, x_down = dev(x_=wrap(x + 1, NX)), dev(x_=wrap(x - 1, NX))
    z_up, z_down = dev(z_=wrap(z + 1, NZ)), dev(z_=wrap(z - 1, NZ))
    y_others = [dev(yl_=wrap(yl + j, NY)) for j in range(1, NY)]
    partner = dev(yh_=1 - yh)

    index_of = {}
    started = []

    def slot_of(key):
        return index_of.setdefault(key, len(index_of))

    def copy_of(key, src, dst, where):
        i = slot_of(key)
        return pltpu.make_async_remote_copy(
            src_ref=src, dst_ref=dst, send_sem=send_sems.at[i], recv_sem=recv_sems.at[i],
            device_id=where, device_id_type=MESH,
        )

    def send(key, src, where, dst=None):
        copy = copy_of(key, src, src if dst is None else dst, where)
        copy.start()
        started.append(copy)

    def recv(key, dst):
        copy_of(key, dst, dst, sibling).wait_recv()

    barrier = pltpu.get_barrier_semaphore()
    for where in [sibling, x_up, x_down, z_up, z_down, partner] + y_others:
        pl.semaphore_signal(barrier, inc=1, device_id=where, device_id_type=MESH)
    pl.semaphore_wait(barrier, 6 + len(y_others))

    wsrc[0] = wq[...]
    wsrc[1, :, 0:hd] = wk[...]
    wsrc[1, :, hd : 2 * hd] = wv[...]
    send("W sibling", wsrc.at[1 - c], sibling, wst)

    def token_block(zz, yy, part):
        return tok.at[
            pl.ds(pl.multiple_of((zz * NH + yy) * own_rows, own_rows), own_rows),
            pl.ds(part * half_width, half_width),
        ]

    def token_key(group, way, distance, part):
        return ("T", group, way, distance, part)

    def token_own(group):
        yy = yh if group == 0 else 1 - yh
        for part in range(2):
            if group == 1:
                recv(("TP", part), token_block(z, yy, part))
            block = token_block(z, yy, part)
            send(token_key(group, "u", 1, part), block, z_up)
            send(token_key(group, "d", 1, part), block, z_down)

    def token_step(group, distance):
        yy = yh if group == 0 else 1 - yh
        for part in range(2):
            for way, sign, where in (("u", -1, z_up), ("d", 1, z_down)):
                if distance == 4 and part != (0 if way == "u" else 1):
                    continue
                block = token_block(wrap(z + sign * distance, NZ), yy, part)
                recv(token_key(group, way, distance, part), block)
                if distance < 3 or (distance == 3 and part == (0 if way == "u" else 1)):
                    send(token_key(group, way, distance + 1, part), block, where)

    normed = unit_rms(hid[...].astype(F32)) * ing[...]
    tok[pl.ds(pl.multiple_of(head * own_rows, own_rows), own_rows), :] = normed.astype(BF16)
    token_own(0)
    for part in range(2):
        send(("TP", part), token_block(z, yh, part), partner)

    class Gather:
        def __init__(self, name, block, part):
            self.name, self.block, self.part = name, block, part

        def at(self, dx, i, core):
            return self.block(wrap(x + dx, NX), wrap(yl - i, NY), core)

        def half(self, dx, i, k):
            return self.part(wrap(x + dx, NX), wrap(yl - i, NY), c, k)

        def own(self):
            block = self.at(0, 0, c)
            send((self.name, "u", 0), block, x_up)
            send((self.name, "d", 0), block, x_down)
            for j in range(1, NY):
                send((self.name, "y", j), block, y_others[j - 1])
            send((self.name, "s", 0, 0), block, sibling)

        def y_step(self, i):
            block = self.at(0, i, c)
            recv((self.name, "y", i), block)
            send((self.name, "u", i), block, x_up)
            send((self.name, "d", i), block, x_down)
            send((self.name, "s", 0, i), block, sibling)

        def x_step(self, i):
            block = self.at(-1, i, c)
            recv((self.name, "u", i), block)
            send((self.name, "ou", i), self.half(-1, i, 0), x_up)
            send((self.name, "s", -1, i), block, sibling)
            block = self.at(1, i, c)
            recv((self.name, "d", i), block)
            send((self.name, "od", i), self.half(1, i, 1), x_down)
            send((self.name, "s", 1, i), block, sibling)

        def o_step(self, i):
            recv((self.name, "ou", i), self.half(2, i, 0))
            recv((self.name, "od", i), self.half(2, i, 1))
            send((self.name, "s", 2, i), self.at(2, i, c), sibling)

        def arrived(self, dx):
            for i in range(NY):
                recv((self.name, "s", dx, i), self.at(dx, i, 1 - c))

    first = 176

    def w_part(ref, core, chip, k):
        start, size = (0, first) if k == 0 else (first, pair - first)
        return ref.at[core, pl.ds(pl.multiple_of(chip * pair + start, 16), size)]

    def w_whole(ref, core, chip):
        return ref.at[core, pl.ds(pl.multiple_of(chip * pair, 16), pair)]

    def c_rows(chip, core, start, size):
        return kvb.at[pl.ds(pl.multiple_of((chip * NC + core) * block_rows + start, 16), size)]

    gather_w = Gather(
        "W",
        lambda xx, yy, core: w_whole(wb, core, xx * NY + yy),
        lambda xx, yy, core, k: w_part(wb, core, xx * NY + yy, k),
    )
    gather_c = Gather(
        "C",
        lambda xx, yy, core: c_rows(xx * NY + yy, core, 0, block_rows),
        lambda xx, yy, core, k: c_rows(xx * NY + yy, core, k * (block_rows // 2), block_rows // 2),
    )
    gather_o = Gather(
        "O",
        lambda xx, yy, core: w_whole(wob, core, xx * NY + yy),
        lambda xx, yy, core, k: w_part(wob, core, xx * NY + yy, k),
    )
    chip = x * NY + yl

    def join_pair(mine, other):
        mine, other = mine.astype(F32), other.astype(F32)
        upper = jnp.where(c == 0, mine, other)
        lower = jnp.where(c == 0, other, mine)
        return jnp.concatenate([upper, lower], axis=0).astype(BF16)

    recv("W sibling", wst)
    wb[c, pl.ds(pl.multiple_of(chip * pair, 16), pair), :] = join_pair(wsrc[c], wst[...])
    gather_w.own()

    slot_block = table[roll]
    pick = lax.broadcasted_iota(jnp.int32, (slots, hd), 0) == slot_block
    start_cos = jnp.sum(jnp.where(pick, block_cos[...], 0.0), axis=0, keepdims=True)
    start_sin = jnp.sum(jnp.where(pick, block_sin[...], 0.0), axis=0, keepdims=True)
    lane = lax.broadcasted_iota(jnp.int32, (1, hd), 1)
    sign = jnp.where(lane < hd // 2, -1.0, 1.0)
    cosine = start_cos * row_cos[...] - start_sin * row_sin[...]
    sine = (start_sin * row_cos[...] + start_cos * row_sin[...]) * sign
    own_cache = pl.ds(pl.multiple_of(roll * block_rows, 16), block_rows)
    kvb[own_cache, 0:hd] = rotate(ck[...].astype(F32), cosine, sine).astype(BF16)
    kvb[own_cache, hd : 2 * hd] = cv[...]

    rows_i = lax.broadcasted_iota(jnp.int32, (2 * hd, 2 * hd), 0)
    cols_i = lax.broadcasted_iota(jnp.int32, (2 * hd, 2 * hd), 1)
    identity = jnp.where(rows_i == cols_i, 1.0, 0.0).astype(BF16)
    turned = lax.dot_general(
        wo[...], identity, (((0,), (0,)), ((), ())), preferred_element_type=F32
    ).astype(BF16)
    osrc[0] = turned[:, 0:hd]
    osrc[1] = turned[:, hd : 2 * hd]
    send("O sibling", osrc.at[1 - c], sibling, ost)

    token_step(0, 1)
    gather_w.y_step(1)
    gather_w.y_step(2)
    token_step(0, 2)
    gather_w.y_step(3)
    token_own(1)
    token_step(0, 3)
    gather_w.x_step(0)
    gather_c.own()
    token_step(0, 4)
    token_step(1, 1)
    gather_w.x_step(1)
    gather_c.y_step(1)
    gather_w.x_step(2)
    gather_c.y_step(2)
    token_step(1, 2)
    gather_w.x_step(3)
    gather_c.y_step(3)
    recv("O sibling", ost)
    wob[c, pl.ds(pl.multiple_of(chip * pair, 16), pair), :] = join_pair(osrc[c], ost[...])
    gather_o.own()
    for i in range(NY):
        gather_w.o_step(i)
        gather_c.x_step(i)
    token_step(1, 3)
    for i in range(1, NY):
        gather_o.y_step(i)
    token_step(1, 4)
    for dx in (0, -1, 1, 2):
        gather_w.arrived(dx)

    depth = 768
    proj[...] = jnp.zeros_like(proj)

    def project(step, carry):
        at = pl.ds(pl.multiple_of(step * depth, depth), depth)
        rows = tok[:, at]
        proj[:, 0 : 2 * hd] += jnp.dot(rows, wb[0, at, :], preferred_element_type=F32)
        proj[:, 2 * hd : 4 * hd] += jnp.dot(rows, wb[1, at, :], preferred_element_type=F32)
        return carry

    lax.fori_loop(0, width // depth, project, 0)
    for g in range(2):
        query = unit_rms(proj[:, g * hd : (g + 1) * hd]) * qg[...]
        queries[pl.ds(g * seg, seg), :] = rotate(query, seg_cos[...], seg_sin[...]).astype(BF16)
    key = unit_rms(proj[:, 2 * hd : 3 * hd]) * kg[...]
    seg_key = rotate(key, seg_cos[...], seg_sin[...]).astype(BF16)
    seg_value = proj[:, 3 * hd : 4 * hd].astype(BF16)

    for i in range(NY):
        gather_c.o_step(i)
        gather_o.x_step(i)

    scale = 1.0 / QSCALE**0.5
    length = length_ref[0]
    scores = nt_dot(queries[...], seg_key) * scale
    row_t = lax.rem(lax.broadcasted_iota(jnp.int32, scores.shape, 0), seg)
    col_t = lax.broadcasted_iota(jnp.int32, scores.shape, 1)
    scores = jnp.where((col_t <= row_t) & (col_t < length), scores, -1e30)
    best = jnp.max(scores, axis=1, keepdims=True)
    weights = jnp.exp(scores - best)
    row_best[...] = jnp.broadcast_to(best, row_best.shape)
    row_total[...] = jnp.broadcast_to(jnp.sum(weights, axis=1, keepdims=True), row_total.shape)
    att_acc[...] = jnp.dot(weights.astype(BF16), seg_value, preferred_element_type=F32)

    keys_per = 640
    group_rows = NY * NC * block_rows

    for dx in (0, -1, 1, 2):
        gather_c.arrived(dx)
        group_start = wrap(x + dx, NX) * group_rows

        def attend(step, carry, group_start=group_start):
            at = pl.ds(pl.multiple_of(group_start + step * keys_per, 16), keys_per)
            scores = nt_dot(queries[...], kvb[at, 0:hd]) * scale
            old_best = row_best[:, 0:1]
            best = jnp.maximum(old_best, jnp.max(scores, axis=1, keepdims=True))
            rescale = jnp.exp(old_best - best)
            weights = jnp.exp(scores - best)
            row_best[...] = jnp.broadcast_to(best, row_best.shape)
            row_total[...] = row_total[...] * rescale + jnp.sum(weights, axis=1, keepdims=True)
            att_acc[...] = att_acc[...] * rescale + jnp.dot(
                weights.astype(BF16), kvb[at, hd : 2 * hd], preferred_element_type=F32
            )
            return carry

        lax.fori_loop(0, group_rows // keys_per, attend, 0)

    for i in range(NY):
        gather_o.o_step(i)
    combined = (att_acc[...] / row_total[...]).astype(BF16)
    attended = jnp.concatenate([combined[0:seg], combined[seg : 2 * seg]], axis=1)
    for dx in (0, -1, 1, 2):
        gather_o.arrived(dx)

    span = NH * own_rows

    def term_at(dz, p):
        return (
            pl.ds(pl.multiple_of(wrap(z + dz, NZ) * span, span), span),
            pl.ds(p * piece, piece),
        )

    def make_term(p):
        at = pl.ds(p * piece, piece)
        columns = jnp.concatenate([wob[0, at, :], wob[1, at, :]], axis=1)
        term[:, at] = nt_dot(attended, columns).astype(BF16)

    def ring_step(way, k, p):
        sign, where, buf = (1, z_up, ru) if way == "u" else (-1, z_down, rd)
        at = term_at(sign * (4 - k), p)
        first_piece = (p < PIECES // 2) == (way == "u")
        if k >= 2 or (k == 1 and first_piece):
            recv(("R", way, k - 1, p), buf.at[k - 1, p])
            term[at] = (term[at].astype(F32) + buf[k - 1, p].astype(F32)).astype(BF16)
        send(("R", way, k, p), term.at[at], where, buf.at[k, p])

    up_first, down_first = [0, 1, 2], [3, 4, 5]
    for pu, pd in zip(up_first, down_first):
        make_term(pu)
        ring_step("u", 0, pu)
        make_term(pd)
        ring_step("d", 0, pd)
    for pu, pd in zip(down_first, up_first):
        ring_step("u", 1, pu)
        ring_step("d", 1, pd)
    for pu, pd in zip(up_first, down_first):
        ring_step("u", 1, pu)
        ring_step("d", 1, pd)
    for k in (2, 3):
        for pu, pd in zip(down_first + up_first, up_first + down_first):
            ring_step("u", k, pu)
            ring_step("d", k, pd)
    for p in (0, 3, 1, 4, 2, 5):
        recv(("R", "u", 3, p), ru.at[3, p])
        recv(("R", "d", 3, p), rd.at[3, p])
        at = pl.ds(p * piece, piece)
        total[:, at] = (
            term[term_at(0, p)].astype(F32) + ru[3, p].astype(F32) + rd[3, p].astype(F32)
        )
        theirs = pl.ds(pl.multiple_of((1 - yh) * own_rows, own_rows), own_rows)
        ysend[p] = total[theirs, at].astype(BF16)
        send(("Y", p), ysend.at[p], partner, yrecv.at[p])
    mine = pl.ds(pl.multiple_of(yh * own_rows, own_rows), own_rows)
    sums = []
    for p in range(PIECES):
        recv(("Y", p), yrecv.at[p])
        sums.append(total[mine, pl.ds(p * piece, piece)] + yrecv[p].astype(F32))
    branch = unit_rms(jnp.concatenate(sums, axis=1)) * og[...]
    row_i = lax.broadcasted_iota(jnp.int32, (own_rows, 1), 0)
    masked = jnp.zeros((own_rows, 1), jnp.int32)
    for t in range(own_rows):
        masked = jnp.where(row_i == t, tool[0, t], masked)
    keep = jnp.where((head * own_rows + row_i < length) & (masked == 0), 1.0, 0.0)
    out[...] = ((hid[...].astype(F32) + branch) * keep).astype(BF16)

    for copy in started:
        copy.wait_send()


def on_device(
    hidden, in_gain, w_query, w_key, w_value, q_gain, k_gain, w_out, out_gain,
    cache_keys, cache_values, block_table, seg_length, tool_mask,
):
    own_rows, width = hidden.shape[1:]
    hd = q_gain.shape[0]
    slots = block_table.shape[0]
    block_rows = cache_keys.shape[0]
    seg = own_rows * NZ * NH
    shard = w_query.shape[0]
    half = hd // 2
    block_cos, block_sin = rope_rows(np.arange(slots) * block_rows, hd)
    row_cos, row_sin = rope_rows(np.arange(block_rows), hd)
    block_sin = np.concatenate([block_sin[:, half:], block_sin[:, half:]], axis=1)
    row_sin = np.concatenate([row_sin[:, half:], row_sin[:, half:]], axis=1)
    seg_cos, seg_sin = rope_rows(slots * block_rows + np.arange(seg), hd)
    piece = width // PIECES
    span = NH * own_rows
    vmem = pl.BlockSpec(memory_space=pltpu.VMEM)
    smem = pl.BlockSpec(memory_space=pltpu.SMEM)
    copies = 200
    result = pl.pallas_call(
        kernel,
        out_shape=jax.ShapeDtypeStruct((own_rows, width), BF16),
        in_specs=[vmem] * 17 + [smem] * 3,
        out_specs=vmem,
        scratch_shapes=[
            pltpu.VMEM((seg, width), BF16),
            pltpu.VMEM((2, width, 2 * hd), BF16),
            pltpu.VMEM((slots * block_rows, 2 * hd), BF16),
            pltpu.VMEM((2, width, hd), BF16),
            pltpu.VMEM((2, shard, 2 * hd), BF16),
            pltpu.VMEM((shard, 2 * hd), BF16),
            pltpu.VMEM((2, shard, hd), BF16),
            pltpu.VMEM((shard, hd), BF16),
            pltpu.VMEM((seg, width), BF16),
            pltpu.VMEM((4, PIECES, span, piece), BF16),
            pltpu.VMEM((4, PIECES, span, piece), BF16),
            pltpu.VMEM((PIECES, own_rows, piece), BF16),
            pltpu.VMEM((PIECES, own_rows, piece), BF16),
            pltpu.VMEM((span, width), F32),
            pltpu.VMEM((seg, 4 * hd), F32),
            pltpu.VMEM((2 * seg, hd), BF16),
            pltpu.VMEM((2 * seg, hd), F32),
            pltpu.VMEM((2 * seg, hd), F32),
            pltpu.VMEM((2 * seg, hd), F32),
            pltpu.SemaphoreType.DMA((copies,)),
            pltpu.SemaphoreType.DMA((copies,)),
        ],
        compiler_params=pltpu.CompilerParams(
            collective_id=0, has_side_effects=True, vmem_limit_bytes=56 * 2**20
        ),
    )(
        hidden[0], in_gain[None], w_query, w_key, w_value, q_gain[None], k_gain[None], w_out,
        out_gain[None], cache_keys, cache_values,
        block_cos, block_sin, row_cos, row_sin, seg_cos, seg_sin,
        block_table, seg_length, tool_mask,
    )
    return result[None]


def solution(mesh):
    return jax.shard_map(
        on_device,
        mesh=mesh,
        in_specs=(
            P("roll", "head", None),
            P(),
            P("roll", "head"),
            P("roll", "head"),
            P("roll", "head"),
            P(),
            P(),
            P("head", "roll"),
            P(),
            P("roll", "head"),
            P("roll", "head"),
            P(),
            P("roll"),
            P("roll", "head"),
        ),
        out_specs=P("roll", "head", None),
        check_vma=False,
    )
```

time: 754 us -> 131 us (0.17)
  waiting for transfers between devices: 673 us -> 0 us
  Pallas kernels: 0 us -> 125 us
  other arithmetic: 34.3 us -> 0 us
  matrix products: 24.1 us -> 0 us
  between operations: 14.4 us -> 0.7 us
    all_gather x7 -> x0, waiting for transfers between devices: 442 us -> none  [the longest x1 106 us: on_device(): tokens_all = lax.all_gather(normed, 'head', axis=0, tiled=True)]
    reduce_scatter x1 -> x0, waiting for transfers between devices: 227 us -> none  [on_device(): lax.psum_scatter(jnp.dot(attended, out_full, preferred_element_type=jnp.f...]
    pallas_call x0 -> x1, Pallas kernels: none -> 125 us  [on_device(): pl.pallas_call(kernel, out_shape=jax.ShapeDtypeStruct((own_rows, width),...]
    dot_general x15 -> x0, matrix products: 24.1 us -> none  [the longest x6 10.6 us: merge_scores(): jnp.einsum('grtn,ngd->grtd', weights.astype(jnp.bfloat16), value_block, p...]
    concatenate x7 -> x0, other arithmetic: 13.2 us -> none  [rotate(): jnp.concatenate([first_half * cosine_table - second_half * sine_table, se...]
    convert_element_type x13 -> x0, other arithmetic: 9.59 us -> none  [the longest x5 4.96 us: attend_block(): key_rows.astype(jnp.float32).reshape(row_count, kv_local, head_dim)]
  transfers between devices with their start and end apart: 8 -> 0, of which waited for: 8 -> 0; matrix products, arithmetic and copies ran while one was open for 7% -> 0% of each run, Pallas kernels for 0% -> 0%
where the time goes in v1:
time: 131 us
  Pallas kernels  125 us (95%)
  local copies, waits for them, and re-layouts  5.07 us (4%)
    pallas_call x1, Pallas kernels, on_device(): pl.pallas_call(kernel, out_shape=jax.ShapeDtypeStruct((own_rows, width),...  125 us

profile of v1, /device:TPU:1, one launch (start us, length us, event | category | flops | bytes accessed | tf_op | source)
XLA Modules:
  0.0 131.1 jit_solution(15073707348430573900)
XLA Ops:
  0.0 0.0 copy-start
  0.7 1.4 %broadcast_in_dim.15.ing = f32[1,5376]{1,0:T(1,128)} reshape(f32[5376]{0:T(1024)} %param.21) | data formatting | bytes 43008 | tf_op jit(solution)/shard_map/broadcast_in_dim | solution.py:464
  2.0 1.4 %broadcast_in_dim.18.og = f32[1,5376]{1,0:T(1,128)} reshape(f32[5376]{0:T(1024)} %param.28) | data formatting | bytes 43008 | tf_op jit(solution)/shard_map/broadcast_in_dim | solution.py:465
  3.4 0.0 copy-done
  3.4 0.8 copy.21.wo
  4.2 125.3 %shard_map.190 = bf16[16,5376]{1,0:T(8,128)(2,1)} custom-call(bf16[16,5376]{1,0:T(8,128)(2,1)} %bitcast.5, f32[1,5376]{1,0:T(1,128)} %broadcast_in_dim.15.ing, bf16[168,256]{1,0:T(8,128)(2,1)} %wq.1, bf16[168,128]{1,0:T(8,128)(2,1)} %wk.1, bf16[168,128]{1,0:T(8,128)(2,1)} %wv.1, f32[1,128]{1,0:T(1,128)} %bitcast.6, f32[1,128]{1,0:T(1,128)} %bitcast.7, ...), custom_call_target="tpu_custom_call" | custom-call | tf_op jit(solution)/shard_map/pallas_call | solution.py:432
  129.5 1.6 %copy.24 = bf16[1,16,5376]{2,1,0:T(8,128)(2,1)} copy(bf16[1,16,5376]{2,1,0:T(8,128)(2,1)} %bitcast.4) | data formatting | bytes 344064
Async XLA Ops:
  0.0 3.4 %copy-start = (bf16[256,168]{0,1:T(8,128)(2,1)S(1)}, bf16[256,168]{0,1:T(8,128)(2,1)}, u32[]{:S(2)}) copy-start(bf16[256,168]{0,1:T(8,128)(2,1)} %param.27) | copy-start | bytes 258052

commit v2 on v1

v2 whole, which is shorter than its diff:
```python
import math

import jax
import jax.numpy as jnp
import numpy as np
from jax import lax
from jax.experimental import pallas as pl
from jax.experimental.pallas import tpu as pltpu
from jax.sharding import PartitionSpec as P

QSCALE = 168
EPSILON = 1e-06
ROPE_BASE = 1000000.0
MESH = pl.DeviceIdType.MESH
F32 = jnp.float32
BF16 = jnp.bfloat16

NX, NY, NC, NZ, NH = 4, 4, 2, 8, 2
PIECES = 6

(
    TOKENS, TOKENS_OWN, READY, PROJECT, SEGMENT, ATTEND, CLOSE, TERM, RING, LAST, FINISH,
    OWN_Y, OWN_X, FROM_Y, FROM_X, FROM_OPPOSITE, ARRIVED,
) = range(17)
UP, DOWN = range(2)
QKV, CACHE, OUT = range(3)
ORDER = (
    (OWN_Y, CACHE, 0), (TOKENS, 0, DOWN, 1, 0), (OWN_X, CACHE, 0), (FROM_Y, QKV, 1, 0),
    (TOKENS, 0, UP, 1, 1), (FROM_X, QKV, DOWN, 0, 1), (FROM_Y, QKV, 1, 1),
    (FROM_X, CACHE, DOWN, 0, 0), (TOKENS, 0, UP, 2, 1), (READY,), (OWN_X, OUT, 0),
    (FROM_X, QKV, UP, 1, 0), (FROM_Y, CACHE, 1, 0), (OWN_Y, CACHE, 1), (FROM_X, QKV, UP, 0, 0),
    (TOKENS, 0, UP, 1, 0), (FROM_X, CACHE, UP, 0, 0), (OWN_X, OUT, 1), (TOKENS, 0, DOWN, 1, 1),
    (TOKENS, 0, DOWN, 2, 0), (OWN_X, CACHE, 1), (FROM_X, QKV, DOWN, 1, 1), (FROM_X, QKV, UP, 0, 1),
    (FROM_Y, QKV, 2, 1), (FROM_OPPOSITE, QKV, DOWN, 0), (TOKENS_OWN, 1), (FROM_Y, QKV, 2, 0),
    (FROM_X, QKV, DOWN, 1, 0), (FROM_Y, CACHE, 1, 1), (TOKENS, 0, DOWN, 2, 1), (FROM_Y, QKV, 3, 0),
    (OWN_Y, OUT, 1), (TOKENS, 1, UP, 1, 0), (TOKENS, 1, DOWN, 1, 1), (TOKENS, 0, UP, 2, 0),
    (FROM_X, CACHE, DOWN, 0, 1), (FROM_Y, QKV, 3, 1), (FROM_X, QKV, DOWN, 2, 1),
    (TOKENS, 1, UP, 1, 1), (FROM_Y, CACHE, 3, 0), (OWN_Y, OUT, 0), (TOKENS, 1, DOWN, 1, 0),
    (FROM_OPPOSITE, QKV, UP, 0), (FROM_Y, CACHE, 2, 1), (FROM_X, OUT, UP, 0, 1),
    (TOKENS, 0, DOWN, 3, 1), (TOKENS, 1, UP, 2, 0), (TOKENS, 1, DOWN, 2, 1), (FROM_Y, OUT, 1, 1),
    (FROM_X, QKV, UP, 2, 0), (FROM_Y, CACHE, 3, 1), (TOKENS, 0, UP, 3, 0), (TOKENS, 1, DOWN, 2, 0),
    (FROM_X, QKV, UP, 2, 1), (FROM_X, QKV, DOWN, 2, 0), (TOKENS, 1, UP, 2, 1),
    (FROM_X, QKV, UP, 3, 0), (FROM_X, QKV, DOWN, 3, 1), (TOKENS, 1, UP, 3, 0),
    (FROM_X, QKV, UP, 1, 1), (FROM_OPPOSITE, QKV, UP, 1), (TOKENS, 0, DOWN, 4, 1),
    (FROM_Y, OUT, 2, 1), (FROM_Y, OUT, 3, 1), (TOKENS, 1, DOWN, 3, 1), (FROM_Y, OUT, 1, 0),
    (FROM_X, QKV, UP, 3, 1), (FROM_Y, OUT, 2, 0), (FROM_Y, CACHE, 2, 0), (FROM_X, OUT, DOWN, 0, 1),
    (FROM_X, CACHE, DOWN, 2, 1), (FROM_X, CACHE, DOWN, 1, 1), (FROM_X, QKV, DOWN, 0, 0),
    (FROM_OPPOSITE, CACHE, DOWN, 0), (FROM_OPPOSITE, QKV, DOWN, 1), (FROM_X, OUT, UP, 1, 1),
    (ARRIVED, QKV, 0), (FROM_OPPOSITE, QKV, DOWN, 2), (FROM_X, CACHE, UP, 3, 0),
    (FROM_X, QKV, DOWN, 3, 0), (FROM_X, CACHE, UP, 1, 0), (TOKENS, 0, DOWN, 3, 0),
    (TOKENS, 0, UP, 4, 0), (FROM_X, CACHE, DOWN, 1, 0), (FROM_Y, OUT, 3, 0),
    (FROM_OPPOSITE, QKV, UP, 2), (FROM_OPPOSITE, QKV, DOWN, 3), (TOKENS, 0, UP, 3, 1),
    (FROM_X, CACHE, UP, 3, 1), (FROM_X, OUT, DOWN, 0, 0), (FROM_X, OUT, UP, 0, 0),
    (FROM_X, CACHE, UP, 0, 1), (FROM_OPPOSITE, QKV, UP, 3), (FROM_X, CACHE, UP, 2, 1),
    (FROM_X, OUT, DOWN, 1, 1), (TOKENS, 1, DOWN, 3, 0), (FROM_X, CACHE, DOWN, 3, 0),
    (ARRIVED, QKV, 1), (FROM_X, CACHE, UP, 1, 1), (TOKENS, 1, UP, 3, 1),
    (FROM_X, CACHE, DOWN, 3, 1), (ARRIVED, OUT, 0), (TOKENS, 1, UP, 4, 0), (FROM_X, OUT, UP, 2, 1),
    (ARRIVED, QKV, -1), (TOKENS, 1, DOWN, 4, 1), (ARRIVED, QKV, 2), (PROJECT,), (SEGMENT, 0),
    (ARRIVED, CACHE, 0), (FROM_X, OUT, UP, 1, 0), (FROM_X, CACHE, UP, 2, 0),
    (FROM_X, OUT, DOWN, 3, 1), (FROM_X, OUT, UP, 3, 1), (ATTEND, 0, 0), (FROM_X, OUT, DOWN, 2, 1),
    (FROM_OPPOSITE, CACHE, UP, 1), (FROM_X, OUT, DOWN, 1, 0), (FROM_OPPOSITE, CACHE, UP, 3),
    (FROM_X, OUT, DOWN, 2, 0), (FROM_X, OUT, UP, 2, 0), (ARRIVED, CACHE, -1),
    (FROM_OPPOSITE, CACHE, UP, 0), (FROM_X, OUT, UP, 3, 0), (FROM_X, CACHE, DOWN, 2, 0),
    (ATTEND, 0, -1), (FROM_OPPOSITE, CACHE, DOWN, 1), (FROM_X, OUT, DOWN, 3, 0),
    (FROM_OPPOSITE, OUT, DOWN, 1), (FROM_OPPOSITE, CACHE, DOWN, 2), (ARRIVED, CACHE, 1),
    (FROM_OPPOSITE, OUT, UP, 0), (FROM_OPPOSITE, CACHE, UP, 2), (ARRIVED, OUT, -1),
    (FROM_OPPOSITE, OUT, UP, 1), (FROM_OPPOSITE, OUT, DOWN, 0), (ARRIVED, OUT, 1),
    (FROM_OPPOSITE, CACHE, DOWN, 3), (ATTEND, 0, 1), (FROM_OPPOSITE, OUT, UP, 3),
    (FROM_OPPOSITE, OUT, UP, 2), (FROM_OPPOSITE, OUT, DOWN, 3), (ARRIVED, CACHE, 2),
    (FROM_OPPOSITE, OUT, DOWN, 2), (ATTEND, 0, 2), (ARRIVED, OUT, 2), (CLOSE, 0), (TERM, 0, 0),
    (RING, 0, UP, 0, 0), (TERM, 0, 3), (RING, 0, DOWN, 0, 3), (TERM, 0, 1), (RING, 0, UP, 0, 1),
    (TERM, 0, 4), (RING, 0, DOWN, 0, 4), (TERM, 0, 2), (RING, 0, UP, 0, 2), (TERM, 0, 5),
    (RING, 0, DOWN, 0, 5), (RING, 0, UP, 1, 3), (RING, 0, DOWN, 1, 0), (RING, 0, UP, 1, 4),
    (RING, 0, DOWN, 1, 1), (RING, 0, UP, 1, 5), (RING, 0, DOWN, 1, 2), (SEGMENT, 1), (ATTEND, 1, 0),
    (RING, 0, UP, 1, 0), (RING, 0, DOWN, 1, 3), (RING, 0, UP, 1, 1), (RING, 0, DOWN, 1, 4),
    (RING, 0, UP, 1, 2), (RING, 0, DOWN, 1, 5), (ATTEND, 1, -1), (ATTEND, 1, 1),
    (RING, 0, UP, 2, 3), (RING, 0, DOWN, 2, 0), (RING, 0, UP, 2, 4), (RING, 0, DOWN, 2, 1),
    (RING, 0, UP, 2, 5), (RING, 0, DOWN, 2, 2), (RING, 0, UP, 2, 0), (RING, 0, DOWN, 2, 3),
    (RING, 0, UP, 2, 1), (RING, 0, DOWN, 2, 4), (RING, 0, UP, 2, 2), (RING, 0, DOWN, 2, 5),
    (ATTEND, 1, 2), (CLOSE, 1), (RING, 0, UP, 3, 3), (RING, 0, DOWN, 3, 0), (RING, 0, UP, 3, 4),
    (RING, 0, DOWN, 3, 1), (RING, 0, UP, 3, 5), (RING, 0, DOWN, 3, 2), (RING, 0, UP, 3, 0),
    (RING, 0, DOWN, 3, 3), (RING, 0, UP, 3, 1), (RING, 0, DOWN, 3, 4), (RING, 0, UP, 3, 2),
    (RING, 0, DOWN, 3, 5), (TERM, 1, 0), (RING, 1, UP, 0, 0), (TERM, 1, 3), (RING, 1, DOWN, 0, 3),
    (TERM, 1, 1), (RING, 1, UP, 0, 1), (TERM, 1, 4), (RING, 1, DOWN, 0, 4), (TERM, 1, 2),
    (RING, 1, UP, 0, 2), (TERM, 1, 5), (RING, 1, DOWN, 0, 5), (RING, 1, UP, 1, 3),
    (RING, 1, DOWN, 1, 0), (RING, 1, UP, 1, 4), (RING, 1, DOWN, 1, 1), (RING, 1, UP, 1, 5),
    (RING, 1, DOWN, 1, 2), (LAST, 0, 0), (LAST, 0, 3), (LAST, 0, 1), (LAST, 0, 4), (LAST, 0, 2),
    (LAST, 0, 5), (RING, 1, UP, 1, 0), (RING, 1, DOWN, 1, 3), (RING, 1, UP, 1, 1),
    (RING, 1, DOWN, 1, 4), (RING, 1, UP, 1, 2), (RING, 1, DOWN, 1, 5), (RING, 1, UP, 2, 3),
    (RING, 1, DOWN, 2, 0), (RING, 1, UP, 2, 4), (RING, 1, DOWN, 2, 1), (RING, 1, UP, 2, 5),
    (RING, 1, DOWN, 2, 2), (RING, 1, UP, 2, 0), (RING, 1, DOWN, 2, 3), (RING, 1, UP, 2, 1),
    (RING, 1, DOWN, 2, 4), (RING, 1, UP, 2, 2), (RING, 1, DOWN, 2, 5), (RING, 1, UP, 3, 3),
    (RING, 1, DOWN, 3, 0), (RING, 1, UP, 3, 4), (RING, 1, DOWN, 3, 1), (RING, 1, UP, 3, 5),
    (RING, 1, DOWN, 3, 2), (RING, 1, UP, 3, 0), (RING, 1, DOWN, 3, 3), (RING, 1, UP, 3, 1),
    (RING, 1, DOWN, 3, 4), (RING, 1, UP, 3, 2), (RING, 1, DOWN, 3, 5), (LAST, 1, 0), (LAST, 1, 3),
    (LAST, 1, 1), (LAST, 1, 4), (LAST, 1, 2), (LAST, 1, 5), (FINISH,),
)

def rope_rows(positions, head_dim):
    half = head_dim // 2
    inverse = ROPE_BASE ** (-np.arange(half, dtype=np.float64) * 2.0 / head_dim)
    angles = np.asarray(positions, np.float64)[:, None] * inverse[None, :]
    cosine, sine = np.cos(angles), np.sin(angles)
    return (
        np.concatenate([cosine, cosine], axis=1).astype(np.float32),
        np.concatenate([-sine, sine], axis=1).astype(np.float32),
    )


def unit_rms(values):
    mean_square = jnp.mean(values * values, axis=-1, keepdims=True)
    return values * lax.rsqrt(mean_square + EPSILON)


def rotate(values, cosine, signed_sine):
    half = values.shape[-1] // 2
    return values * cosine + pltpu.roll(values, half, axis=1) * signed_sine


def nt_dot(left, right):
    return lax.dot_general(left, right, (((1,), (1,)), ((), ())), preferred_element_type=F32)


def kernel(
    hid_in, ing_in, wq_in, wk_in, wv_in, qg_in, kg_in, wo_in, og_in, ck_in, cv_in, tables_in,
    table, length_ref, tool,
    out,
    hid, ing, og, qg, kg, wo, ck, tables,
    tok, wb, kvb, wob, wsrc, wst, osrc, ost, term, ru, rd, ysend, yrecv, total,
    proj, queries, seg_keys, seg_values, attended, att_acc, row_best, row_total,
    load_sems, send_sems, recv_sems,
):
    roll, head = lax.axis_index("roll"), lax.axis_index("head")
    x, yl, c = lax.div(roll, 8), lax.rem(lax.div(roll, 2), 4), lax.rem(roll, 2)
    z, yh = lax.div(head, 2), lax.rem(head, 2)
    own_rows, width = hid.shape
    slots, shard = table.shape[0], wq_in.shape[0]
    pair = 2 * shard
    block_rows = ck.shape[0]
    hd = qg.shape[1]
    own_cache = pl.ds(pl.multiple_of(roll * block_rows, 16), block_rows)

    loads = {}

    def load(name, src, dst):
        loads[name] = pltpu.make_async_copy(src, dst, load_sems.at[len(loads)])
        loads[name].start()

    def loaded(*names):
        for name in names:
            loads[name].wait()

    load("hid", hid_in, hid)
    load("ing", ing_in, ing)
    load("wq", wq_in, wsrc.at[0])
    load("wk", wk_in, wsrc.at[1, :, pl.ds(0, hd)])
    load("wv", wv_in, wsrc.at[1, :, pl.ds(hd, hd)])
    load("ck", ck_in, ck)
    load("cv", cv_in, kvb.at[own_cache, pl.ds(hd, hd)])
    load("tables", tables_in, tables)
    load("wo", wo_in, wo)
    load("qg", qg_in, qg)
    load("kg", kg_in, kg)
    load("og", og_in, og)
    seg = tok.shape[0]
    half_width = width // 2
    piece = width // PIECES

    def wrap(value, size):
        return lax.rem(value + size, size)

    def dev(x_=x, yl_=yl, c_=c, z_=z, yh_=yh):
        return {"roll": (x_ * NY + yl_) * NC + c_, "head": z_ * NH + yh_}

    sibling = dev(c_=1 - c)
    x_up, x_down = dev(x_=wrap(x + 1, NX)), dev(x_=wrap(x - 1, NX))
    z_up, z_down = dev(z_=wrap(z + 1, NZ)), dev(z_=wrap(z - 1, NZ))
    upper = lax.div(yl, 2)
    inner = yl + upper * (3 - 2 * yl)

    def mirrored(place):
        return place + upper * (3 - 2 * place)

    y_near = [yl, mirrored(1 - inner), mirrored(2), mirrored(3)]
    y_next = dev(yl_=y_near[1])
    y_end, y_middle = dev(yl_=mirrored(0)), dev(yl_=mirrored(2))
    partner = dev(yh_=1 - yh)

    index_of = {}
    started = []

    def slot_of(key):
        return index_of.setdefault(key, len(index_of))

    def copy_of(key, src, dst, where):
        i = slot_of(key)
        return pltpu.make_async_remote_copy(
            src_ref=src, dst_ref=dst, send_sem=send_sems.at[i], recv_sem=recv_sems.at[i],
            device_id=where, device_id_type=MESH,
        )

    def send(key, src, where, dst=None, when=None):
        copy = copy_of(key, src, src if dst is None else dst, where)
        if when is None:
            copy.start()
        else:
            pl.when(when)(copy.start)
        started.append((copy, when))

    def recv(key, dst):
        copy_of(key, dst, dst, sibling).wait_recv()

    barrier = pltpu.get_barrier_semaphore()
    for where in [sibling, x_up, x_down, z_up, z_down, partner, y_next]:
        pl.semaphore_signal(barrier, inc=1, device_id=where, device_id_type=MESH)

    @pl.when(inner == 1)
    def _():
        pl.semaphore_signal(barrier, inc=1, device_id=y_middle, device_id_type=MESH)

    loaded("hid", "ing")
    normed = unit_rms(hid[...].astype(F32)) * ing[...].reshape(1, width)
    tok[pl.ds(pl.multiple_of((yh * NZ + z) * own_rows, own_rows), own_rows), :] = normed.astype(BF16)
    loaded("wq", "wk", "wv")
    pl.semaphore_wait(barrier, 7 + inner)

    send("W sibling", wsrc.at[1 - c], sibling, wst)

    def token_block(zz, yy, part):
        return tok.at[
            pl.ds(pl.multiple_of((yy * NZ + zz) * own_rows, own_rows), own_rows),
            pl.ds(part * half_width, half_width),
        ]

    def token_key(group, way, distance, part):
        return ("T", group, way, distance, part)

    def token_own(group):
        yy = yh if group == 0 else 1 - yh
        for part in range(2):
            if group == 1:
                recv(("TP", part), token_block(z, yy, part))
            block = token_block(z, yy, part)
            send(token_key(group, UP, 1, part), block, z_up)
            send(token_key(group, DOWN, 1, part), block, z_down)

    def token_step(group, way, distance, part):
        yy = yh if group == 0 else 1 - yh
        sign, where, last = (-1, z_up, 0) if way == UP else (1, z_down, 1)
        block = token_block(wrap(z + sign * distance, NZ), yy, part)
        recv(token_key(group, way, distance, part), block)
        if distance < 3 or (distance == 3 and part == last):
            send(token_key(group, way, distance + 1, part), block, where)

    def token_partner():
        for part in range(2):
            send(("TP", part), token_block(z, yh, part), partner)

    token_own(0)

    class Gather:
        def __init__(self, name, rows):
            self.name, self.rows = name, rows
            self.steps = {
                OWN_Y: self.own_y, OWN_X: self.own_x, FROM_Y: self.y_step,
                FROM_X: self.x_step, FROM_OPPOSITE: self.o_step, ARRIVED: self.arrived,
            }

        def at(self, dx, i, k, core=c):
            return self.rows(wrap(x + dx, NX) * NY + y_near[i], core, k)

        def own_y(self, k):
            block = self.at(0, 0, k)
            send((self.name, "yn", k), block, y_next)
            send((self.name, "ym", 0, k), block, y_middle, when=inner == 1)

        def own_x(self, k):
            self.spread(0, k)

        def spread(self, i, k):
            block = self.at(0, i, k)
            send((self.name, UP, i, k), block, x_up)
            send((self.name, DOWN, i, k), block, x_down)
            send((self.name, "s", 0, i, k), block, sibling)

        def y_step(self, i, k):
            block = self.at(0, i, k)
            if i == 1:
                recv((self.name, "yn", k), block)
                send((self.name, "ym", 1, k), block, y_middle, when=inner == 1)
            else:
                @pl.when(inner == 1)
                def _():
                    recv((self.name, "ym", i - 2, k), block)

                @pl.when(inner == 0)
                def _():
                    recv((self.name, "ye", i, k), block)

                send((self.name, "ye", i, k), block, y_end, when=inner == 1)
            self.spread(i, k)

        def x_step(self, way, i, k):
            dx, where, last = (-1, x_up, 0) if way == UP else (1, x_down, 1)
            block = self.at(dx, i, k)
            recv((self.name, way, i, k), block)
            if k == last:
                send((self.name, "o", way, i), block, where)
            send((self.name, "s", dx, i, k), block, sibling)

        def o_step(self, way, i):
            k = 0 if way == UP else 1
            block = self.at(2, i, k)
            recv((self.name, "o", way, i), block)
            send((self.name, "s", 2, i, k), block, sibling)

        def arrived(self, dx):
            for i in range(NY):
                for k in range(2):
                    recv((self.name, "s", dx, i, k), self.at(dx, i, k, 1 - c))

    def pair_rows(ref):
        def rows(chip, core, k):
            start, size = pair_parts[k]
            return ref.at[core, pl.ds(pl.multiple_of(chip * pair + start, 16), size)]

        return rows

    def cache_rows(chip, core, k):
        start, size = cache_parts[k]
        return kvb.at[pl.ds(pl.multiple_of((chip * NC + core) * block_rows + start, 16), size)]

    pair_parts = ((0, 176), (176, 160))
    cache_parts = ((0, 80), (80, 80))
    gathers = {
        QKV: Gather("W", pair_rows(wb)),
        CACHE: Gather("C", cache_rows),
        OUT: Gather("O", pair_rows(wob)),
    }
    chip = x * NY + yl

    def join_pair(mine, other):
        mine, other = mine.astype(F32), other.astype(F32)
        upper = jnp.where(c == 0, mine, other)
        lower = jnp.where(c == 0, other, mine)
        return jnp.concatenate([upper, lower], axis=0).astype(BF16)

    recv("W sibling", wst)
    wb[c, pl.ds(pl.multiple_of(chip * pair, 16), pair), :] = join_pair(wsrc[c], wst[...])
    for k in range(2):
        gathers[QKV].own_y(k)
        gathers[QKV].own_x(k)
    token_partner()

    slot_block = table[roll]
    loaded("tables", "ck")
    first_seg = slots + block_rows
    block_cos, block_sin = tables[0:slots, 0:hd], tables[0:slots, hd : 2 * hd]
    row_cos, row_sin = tables[slots:first_seg, 0:hd], tables[slots:first_seg, hd : 2 * hd]
    seg_cos = tables[first_seg : first_seg + seg, 0:hd]
    seg_sin = tables[first_seg : first_seg + seg, hd : 2 * hd]
    pick = lax.broadcasted_iota(jnp.int32, (slots, hd), 0) == slot_block
    start_cos = jnp.sum(jnp.where(pick, block_cos, 0.0), axis=0, keepdims=True)
    start_sin = jnp.sum(jnp.where(pick, block_sin, 0.0), axis=0, keepdims=True)
    lane = lax.broadcasted_iota(jnp.int32, (1, hd), 1)
    sign = jnp.where(lane < hd // 2, -1.0, 1.0)
    cosine = start_cos * row_cos - start_sin * row_sin
    sine = (start_sin * row_cos + start_cos * row_sin) * sign
    kvb[own_cache, 0:hd] = rotate(ck[...].astype(F32), cosine, sine).astype(BF16)
    loaded("cv")

    loaded("wo", "qg", "kg")
    turned = wo[...]
    osrc[0] = turned[:, 0:hd]
    osrc[1] = turned[:, hd : 2 * hd]
    send("O sibling", osrc.at[1 - c], sibling, ost)

    rows = seg // NH

    def project_all():
        depth = 1792
        proj[...] = jnp.zeros_like(proj)

        def project(step, carry):
            at = pl.ds(pl.multiple_of(step * depth, depth), depth)
            tokens = tok[:, at]
            proj[:, 0 : 2 * hd] += jnp.dot(tokens, wb[0, at, :], preferred_element_type=F32)
            proj[:, 2 * hd : 4 * hd] += jnp.dot(tokens, wb[1, at, :], preferred_element_type=F32)
            return carry

        lax.fori_loop(0, width // depth, project, 0)
        for g in range(2):
            query = unit_rms(proj[:, g * hd : (g + 1) * hd]) * qg[...]
            query = rotate(query, seg_cos, seg_sin).astype(BF16)
            for yy in range(NH):
                queries[yy, g * rows : (g + 1) * rows, :] = query[yy * rows : (yy + 1) * rows]
        key = unit_rms(proj[:, 2 * hd : 3 * hd]) * kg[...]
        seg_keys[...] = rotate(key, seg_cos, seg_sin).astype(BF16)
        seg_values[...] = proj[:, 3 * hd : 4 * hd].astype(BF16)

    scale = 1.0 / QSCALE**0.5 / math.log(2.0)
    length = length_ref[0]
    group_y = (1 - yh, yh)

    def exponentials(scores, best):
        return [
            jnp.exp2((scores[:, j : j + hd] - best) * scale) for j in range(0, scores.shape[1], hd)
        ]

    def weighted(weights, values):
        weights = jnp.concatenate([part.astype(BF16) for part in weights], axis=1)
        return jnp.dot(weights, values, preferred_element_type=F32)

    def attend_segment(g):
        scores = nt_dot(queries[group_y[g]], seg_keys[...])
        row = lax.broadcasted_iota(jnp.int32, scores.shape, 0) & (rows - 1)
        row_t = row + (row >> 4) * 16 + group_y[g] * own_rows
        col = lax.broadcasted_iota(jnp.int32, scores.shape, 1)
        col_in = col & (rows - 1)
        col_t = col_in + (col_in >> 4) * 16 + (col >> 7) * own_rows
        scores = jnp.where((col_t <= row_t) & (col_t < length), scores, -1e30)
        best = jnp.broadcast_to(jnp.max(scores, axis=1, keepdims=True), row_best.shape)
        weights = exponentials(scores, best)
        row_best[...] = best
        row_total[...] = sum(weights[1:], weights[0])
        att_acc[...] = weighted(weights, seg_values[...])

    group_rows = NY * NC * block_rows

    def attend_group(g, dx):
        at = pl.ds(pl.multiple_of(wrap(x + dx, NX) * group_rows, 16), group_rows)
        scores = nt_dot(queries[group_y[g]], kvb[at, 0:hd])
        old_best = row_best[...]
        best = jnp.maximum(old_best, jnp.max(scores, axis=1, keepdims=True))
        rescale = jnp.exp2((old_best - best) * scale)
        weights = exponentials(scores, best)
        row_best[...] = best
        row_total[...] = row_total[...] * rescale + sum(weights[1:], weights[0])
        att_acc[...] = att_acc[...] * rescale + weighted(weights, kvb[at, hd : 2 * hd])

    def close_group(g):
        combined = att_acc[...] / jnp.sum(row_total[...], axis=1, keepdims=True)
        combined = combined.astype(BF16)
        for half in range(2):
            attended[g, :, half * hd : (half + 1) * hd] = combined[half * rows : (half + 1) * rows]

    def term_at(g, dz, p):
        return (
            pl.ds(
                pl.multiple_of((group_y[g] * NZ + wrap(z + dz, NZ)) * own_rows, own_rows), own_rows
            ),
            pl.ds(p * piece, piece),
        )

    def make_term(g, p):
        at = pl.ds(p * piece, piece)
        columns = jnp.concatenate([wob[0, at, :], wob[1, at, :]], axis=1)
        place = pl.ds(pl.multiple_of(group_y[g] * rows, rows), rows)
        term[place, at] = nt_dot(attended[g], columns).astype(BF16)

    def ring_step(g, way, k, p):
        sign, where, buf = (1, z_up, ru) if way == UP else (-1, z_down, rd)
        at = term_at(g, sign * (4 - k), p)
        first_piece = (p < PIECES // 2) == (way == UP)
        if k >= 2 or (k == 1 and first_piece):
            recv(("R", g, way, k - 1, p), buf.at[g, k - 1, p])
            term[at] = (term[at].astype(F32) + buf[g, k - 1, p].astype(F32)).astype(BF16)
        send(("R", g, way, k, p), term.at[at], where, buf.at[g, k, p])

    def ring_last(g, p):
        recv(("R", g, UP, 3, p), ru.at[g, 3, p])
        recv(("R", g, DOWN, 3, p), rd.at[g, 3, p])
        summed = (
            term[term_at(g, 0, p)].astype(F32)
            + ru[g, 3, p].astype(F32)
            + rd[g, 3, p].astype(F32)
        )
        if g == 0:
            ysend[p] = summed.astype(BF16)
            send(("Y", p), ysend.at[p], partner, yrecv.at[p])
        else:
            recv(("Y", p), yrecv.at[p])
            total[:, p * piece : (p + 1) * piece] = summed + yrecv[p].astype(F32)

    def finish():
        loaded("og")
        branch = unit_rms(total[...]) * og[...].reshape(1, width)
        row_i = lax.broadcasted_iota(jnp.int32, (own_rows, 1), 0)
        masked = jnp.zeros((own_rows, 1), jnp.int32)
        for t in range(own_rows):
            masked = jnp.where(row_i == t, tool[0, t], masked)
        keep = jnp.where((head * own_rows + row_i < length) & (masked == 0), 1.0, 0.0)
        out[...] = ((hid[...].astype(F32) + branch) * keep).astype(BF16)

    def own_out_ready():
        recv("O sibling", ost)
        wob[c, pl.ds(pl.multiple_of(chip * pair, 16), pair), :] = join_pair(osrc[c], ost[...])

    steps = {
        TOKENS: token_step, TOKENS_OWN: token_own, READY: own_out_ready, PROJECT: project_all,
        SEGMENT: attend_segment, ATTEND: attend_group, CLOSE: close_group,
        TERM: make_term, RING: ring_step, LAST: ring_last, FINISH: finish,
    }

    for op, *what in ORDER:
        if op in steps:
            steps[op](*what)
        else:
            gathers[what[0]].steps[op](*what[1:])

    for copy, when in started:
        if when is None:
            copy.wait_send()
        else:
            pl.when(when)(copy.wait_send)


def on_device(
    hidden, in_gain, w_query, w_key, w_value, q_gain, k_gain, w_out, out_gain,
    cache_keys, cache_values, block_table, seg_length, tool_mask,
):
    own_rows, width = hidden.shape[1:]
    hd = q_gain.shape[0]
    slots = block_table.shape[0]
    block_rows = cache_keys.shape[0]
    seg = own_rows * NZ * NH
    shard = w_query.shape[0]
    half = hd // 2
    block_cos, block_sin = rope_rows(np.arange(slots) * block_rows, hd)
    row_cos, row_sin = rope_rows(np.arange(block_rows), hd)
    block_sin = np.concatenate([block_sin[:, half:], block_sin[:, half:]], axis=1)
    row_sin = np.concatenate([row_sin[:, half:], row_sin[:, half:]], axis=1)
    tokens = np.arange(seg).reshape(NZ, NH, own_rows).transpose(1, 0, 2).reshape(-1)
    seg_cos, seg_sin = rope_rows(slots * block_rows + tokens, hd)
    tables = np.concatenate(
        [
            np.concatenate([block_cos, row_cos, seg_cos], axis=0),
            np.concatenate([block_sin, row_sin, seg_sin], axis=0),
        ],
        axis=1,
    )
    piece = width // PIECES
    vmem = pl.BlockSpec(memory_space=pltpu.VMEM)
    smem = pl.BlockSpec(memory_space=pltpu.SMEM)
    copies = 340
    result = pl.pallas_call(
        kernel,
        out_shape=jax.ShapeDtypeStruct((own_rows, width), BF16),
        in_specs=[pl.BlockSpec(memory_space=pl.ANY)] * 12 + [smem] * 3,
        out_specs=vmem,
        scratch_shapes=[
            pltpu.VMEM((own_rows, width), BF16),
            pltpu.VMEM((width,), F32),
            pltpu.VMEM((width,), F32),
            pltpu.VMEM((1, hd), F32),
            pltpu.VMEM((1, hd), F32),
            pltpu.VMEM((shard, 2 * hd), BF16),
            pltpu.VMEM((block_rows, hd), BF16),
            pltpu.VMEM(tables.shape, F32),
            pltpu.VMEM((seg, width), BF16),
            pltpu.VMEM((2, width, 2 * hd), BF16),
            pltpu.VMEM((slots * block_rows, 2 * hd), BF16),
            pltpu.VMEM((2, width, hd), BF16),
            pltpu.VMEM((2, shard, 2 * hd), BF16),
            pltpu.VMEM((shard, 2 * hd), BF16),
            pltpu.VMEM((2, shard, hd), BF16),
            pltpu.VMEM((shard, hd), BF16),
            pltpu.VMEM((seg, width), BF16),
            pltpu.VMEM((2, 4, PIECES, own_rows, piece), BF16),
            pltpu.VMEM((2, 4, PIECES, own_rows, piece), BF16),
            pltpu.VMEM((PIECES, own_rows, piece), BF16),
            pltpu.VMEM((PIECES, own_rows, piece), BF16),
            pltpu.VMEM((own_rows, width), F32),
            pltpu.VMEM((seg, 4 * hd), F32),
            pltpu.VMEM((NH, seg, hd), BF16),
            pltpu.VMEM((seg, hd), BF16),
            pltpu.VMEM((seg, hd), BF16),
            pltpu.VMEM((2, seg // NH, 2 * hd), BF16),
            pltpu.VMEM((seg, hd), F32),
            pltpu.VMEM((seg, hd), F32),
            pltpu.VMEM((seg, hd), F32),
            pltpu.SemaphoreType.DMA((12,)),
            pltpu.SemaphoreType.DMA((copies,)),
            pltpu.SemaphoreType.DMA((copies,)),
        ],
        compiler_params=pltpu.CompilerParams(
            collective_id=0, has_side_effects=True, vmem_limit_bytes=56 * 2**20
        ),
    )(
        hidden[0], in_gain, w_query, w_key, w_value, q_gain.reshape(1, -1), k_gain.reshape(1, -1),
        w_out.T, out_gain, cache_keys, cache_values, tables,
        block_table, seg_length, tool_mask,
    )
    return result[None]


def solution(mesh):
    return jax.shard_map(
        on_device,
        mesh=mesh,
        in_specs=(
            P("roll", "head", None),
            P(),
            P("roll", "head"),
            P("roll", "head"),
            P("roll", "head"),
            P(),
            P(),
            P("head", "roll"),
            P(),
            P("roll", "head"),
            P("roll", "head"),
            P(),
            P("roll"),
            P("roll", "head"),
        ),
        out_specs=P("roll", "head", None),
        check_vma=False,
    )
```

time: 131 us -> 108 us (0.82)
  Pallas kernels: 125 us -> 105 us
  local copies, waits for them, and re-layouts: 5.07 us -> 1.6 us
    pallas_call x1, Pallas kernels: 125 us -> 105 us  [on_device(): pl.pallas_call(kernel, out_shape=jax.ShapeDtypeStruct((own_rows, width),...]
    broadcast_in_dim x2 -> x0, local copies, waits for them, and re-layouts: 2.71 us -> none  [the longest x1 1.36 us: on_device(): out_gain[None]]
where the time goes in v2:
time: 108 us; the launch traced here: 107 us
  Pallas kernels  105 us (97%)
  local copies, waits for them, and re-layouts  1.6 us (1%)
    pallas_call x1, Pallas kernels, on_device(): pl.pallas_call(kernel, out_shape=jax.ShapeDtypeStruct((own_rows, width),...  105 us

profile of v2, /device:TPU:1, one launch (start us, length us, event | category | flops | bytes accessed | tf_op | source)
XLA Modules:
  0.0 107.4 jit_solution(16147802092401684454)
XLA Ops:
  0.7 105.2 %shard_map.145 = bf16[16,5376]{1,0:T(8,128)(2,1)} custom-call(bf16[16,5376]{1,0:T(8,128)(2,1)} %bitcast.6, f32[5376]{0:T(1024)} %ing_in.1, bf16[168,256]{1,0:T(8,128)(2,1)} %wq_in.1, bf16[168,128]{1,0:T(8,128)(2,1)} %wk_in.1, bf16[168,128]{1,0:T(8,128)(2,1)} %wv_in.1, f32[1,128]{1,0:T(1,128)} %bitcast.8, f32[1,128]{1,0:T(1,128)} %bitcast.9, ...), custom_call_target="tpu_custom_call" | custom-call | tf_op jit(solution)/shard_map/pallas_call | solution.py:546
  105.8 1.6 %copy.18 = bf16[1,16,5376]{2,1,0:T(8,128)(2,1)} copy(bf16[1,16,5376]{2,1,0:T(8,128)(2,1)} %bitcast.5) | data formatting | bytes 344064

commit v3 on v2

--- a/solution.py
+++ b/solution.py
@@ -19,81 +19,80 @@
 PIECES = 6
 
 (
-    TOKENS, TOKENS_OWN, READY, PROJECT, SEGMENT, ATTEND, CLOSE, TERM, RING, LAST, FINISH,
+    TOKENS, TOKENS_OWN, READY, PROJECT, SEGMENT, ATTEND, CLOSE, TERM, RING, SWAP, ADD, LAST, FINISH,
     OWN_Y, OWN_X, FROM_Y, FROM_X, FROM_OPPOSITE, ARRIVED,
-) = range(17)
+    FIRST_OWN_X, FIRST_OWN_Y, FIRST_FROM_X, FIRST_FROM_OPPOSITE, FIRST_FROM_Y,
+) = range(24)
 UP, DOWN = range(2)
 QKV, CACHE, OUT = range(3)
 ORDER = (
-    (OWN_Y, CACHE, 0), (TOKENS, 0, DOWN, 1, 0), (OWN_X, CACHE, 0), (FROM_Y, QKV, 1, 0),
-    (TOKENS, 0, UP, 1, 1), (FROM_X, QKV, DOWN, 0, 1), (FROM_Y, QKV, 1, 1),
-    (FROM_X, CACHE, DOWN, 0, 0), (TOKENS, 0, UP, 2, 1), (READY,), (OWN_X, OUT, 0),
-    (FROM_X, QKV, UP, 1, 0), (FROM_Y, CACHE, 1, 0), (OWN_Y, CACHE, 1), (FROM_X, QKV, UP, 0, 0),
-    (TOKENS, 0, UP, 1, 0), (FROM_X, CACHE, UP, 0, 0), (OWN_X, OUT, 1), (TOKENS, 0, DOWN, 1, 1),
-    (TOKENS, 0, DOWN, 2, 0), (OWN_X, CACHE, 1), (FROM_X, QKV, DOWN, 1, 1), (FROM_X, QKV, UP, 0, 1),
-    (FROM_Y, QKV, 2, 1), (FROM_OPPOSITE, QKV, DOWN, 0), (TOKENS_OWN, 1), (FROM_Y, QKV, 2, 0),
-    (FROM_X, QKV, DOWN, 1, 0), (FROM_Y, CACHE, 1, 1), (TOKENS, 0, DOWN, 2, 1), (FROM_Y, QKV, 3, 0),
-    (OWN_Y, OUT, 1), (TOKENS, 1, UP, 1, 0), (TOKENS, 1, DOWN, 1, 1), (TOKENS, 0, UP, 2, 0),
-    (FROM_X, CACHE, DOWN, 0, 1), (FROM_Y, QKV, 3, 1), (FROM_X, QKV, DOWN, 2, 1),
-    (TOKENS, 1, UP, 1, 1), (FROM_Y, CACHE, 3, 0), (OWN_Y, OUT, 0), (TOKENS, 1, DOWN, 1, 0),
-    (FROM_OPPOSITE, QKV, UP, 0), (FROM_Y, CACHE, 2, 1), (FROM_X, OUT, UP, 0, 1),
-    (TOKENS, 0, DOWN, 3, 1), (TOKENS, 1, UP, 2, 0), (TOKENS, 1, DOWN, 2, 1), (FROM_Y, OUT, 1, 1),
-    (FROM_X, QKV, UP, 2, 0), (FROM_Y, CACHE, 3, 1), (TOKENS, 0, UP, 3, 0), (TOKENS, 1, DOWN, 2, 0),
-    (FROM_X, QKV, UP, 2, 1), (FROM_X, QKV, DOWN, 2, 0), (TOKENS, 1, UP, 2, 1),
-    (FROM_X, QKV, UP, 3, 0), (FROM_X, QKV, DOWN, 3, 1), (TOKENS, 1, UP, 3, 0),
-    (FROM_X, QKV, UP, 1, 1), (FROM_OPPOSITE, QKV, UP, 1), (TOKENS, 0, DOWN, 4, 1),
-    (FROM_Y, OUT, 2, 1), (FROM_Y, OUT, 3, 1), (TOKENS, 1, DOWN, 3, 1), (FROM_Y, OUT, 1, 0),
-    (FROM_X, QKV, UP, 3, 1), (FROM_Y, OUT, 2, 0), (FROM_Y, CACHE, 2, 0), (FROM_X, OUT, DOWN, 0, 1),
-    (FROM_X, CACHE, DOWN, 2, 1), (FROM_X, CACHE, DOWN, 1, 1), (FROM_X, QKV, DOWN, 0, 0),
-    (FROM_OPPOSITE, CACHE, DOWN, 0), (FROM_OPPOSITE, QKV, DOWN, 1), (FROM_X, OUT, UP, 1, 1),
-    (ARRIVED, QKV, 0), (FROM_OPPOSITE, QKV, DOWN, 2), (FROM_X, CACHE, UP, 3, 0),
-    (FROM_X, QKV, DOWN, 3, 0), (FROM_X, CACHE, UP, 1, 0), (TOKENS, 0, DOWN, 3, 0),
-    (TOKENS, 0, UP, 4, 0), (FROM_X, CACHE, DOWN, 1, 0), (FROM_Y, OUT, 3, 0),
-    (FROM_OPPOSITE, QKV, UP, 2), (FROM_OPPOSITE, QKV, DOWN, 3), (TOKENS, 0, UP, 3, 1),
-    (FROM_X, CACHE, UP, 3, 1), (FROM_X, OUT, DOWN, 0, 0), (FROM_X, OUT, UP, 0, 0),
-    (FROM_X, CACHE, UP, 0, 1), (FROM_OPPOSITE, QKV, UP, 3), (FROM_X, CACHE, UP, 2, 1),
-    (FROM_X, OUT, DOWN, 1, 1), (TOKENS, 1, DOWN, 3, 0), (FROM_X, CACHE, DOWN, 3, 0),
-    (ARRIVED, QKV, 1), (FROM_X, CACHE, UP, 1, 1), (TOKENS, 1, UP, 3, 1),
-    (FROM_X, CACHE, DOWN, 3, 1), (ARRIVED, OUT, 0), (TOKENS, 1, UP, 4, 0), (FROM_X, OUT, UP, 2, 1),
-    (ARRIVED, QKV, -1), (TOKENS, 1, DOWN, 4, 1), (ARRIVED, QKV, 2), (PROJECT,), (SEGMENT, 0),
-    (ARRIVED, CACHE, 0), (FROM_X, OUT, UP, 1, 0), (FROM_X, CACHE, UP, 2, 0),
-    (FROM_X, OUT, DOWN, 3, 1), (FROM_X, OUT, UP, 3, 1), (ATTEND, 0, 0), (FROM_X, OUT, DOWN, 2, 1),
-    (FROM_OPPOSITE, CACHE, UP, 1), (FROM_X, OUT, DOWN, 1, 0), (FROM_OPPOSITE, CACHE, UP, 3),
-    (FROM_X, OUT, DOWN, 2, 0), (FROM_X, OUT, UP, 2, 0), (ARRIVED, CACHE, -1),
-    (FROM_OPPOSITE, CACHE, UP, 0), (FROM_X, OUT, UP, 3, 0), (FROM_X, CACHE, DOWN, 2, 0),
-    (ATTEND, 0, -1), (FROM_OPPOSITE, CACHE, DOWN, 1), (FROM_X, OUT, DOWN, 3, 0),
-    (FROM_OPPOSITE, OUT, DOWN, 1), (FROM_OPPOSITE, CACHE, DOWN, 2), (ARRIVED, CACHE, 1),
-    (FROM_OPPOSITE, OUT, UP, 0), (FROM_OPPOSITE, CACHE, UP, 2), (ARRIVED, OUT, -1),
-    (FROM_OPPOSITE, OUT, UP, 1), (FROM_OPPOSITE, OUT, DOWN, 0), (ARRIVED, OUT, 1),
-    (FROM_OPPOSITE, CACHE, DOWN, 3), (ATTEND, 0, 1), (FROM_OPPOSITE, OUT, UP, 3),
-    (FROM_OPPOSITE, OUT, UP, 2), (FROM_OPPOSITE, OUT, DOWN, 3), (ARRIVED, CACHE, 2),
-    (FROM_OPPOSITE, OUT, DOWN, 2), (ATTEND, 0, 2), (ARRIVED, OUT, 2), (CLOSE, 0), (TERM, 0, 0),
-    (RING, 0, UP, 0, 0), (TERM, 0, 3), (RING, 0, DOWN, 0, 3), (TERM, 0, 1), (RING, 0, UP, 0, 1),
-    (TERM, 0, 4), (RING, 0, DOWN, 0, 4), (TERM, 0, 2), (RING, 0, UP, 0, 2), (TERM, 0, 5),
-    (RING, 0, DOWN, 0, 5), (RING, 0, UP, 1, 3), (RING, 0, DOWN, 1, 0), (RING, 0, UP, 1, 4),
-    (RING, 0, DOWN, 1, 1), (RING, 0, UP, 1, 5), (RING, 0, DOWN, 1, 2), (SEGMENT, 1), (ATTEND, 1, 0),
-    (RING, 0, UP, 1, 0), (RING, 0, DOWN, 1, 3), (RING, 0, UP, 1, 1), (RING, 0, DOWN, 1, 4),
-    (RING, 0, UP, 1, 2), (RING, 0, DOWN, 1, 5), (ATTEND, 1, -1), (ATTEND, 1, 1),
-    (RING, 0, UP, 2, 3), (RING, 0, DOWN, 2, 0), (RING, 0, UP, 2, 4), (RING, 0, DOWN, 2, 1),
-    (RING, 0, UP, 2, 5), (RING, 0, DOWN, 2, 2), (RING, 0, UP, 2, 0), (RING, 0, DOWN, 2, 3),
-    (RING, 0, UP, 2, 1), (RING, 0, DOWN, 2, 4), (RING, 0, UP, 2, 2), (RING, 0, DOWN, 2, 5),
-    (ATTEND, 1, 2), (CLOSE, 1), (RING, 0, UP, 3, 3), (RING, 0, DOWN, 3, 0), (RING, 0, UP, 3, 4),
-    (RING, 0, DOWN, 3, 1), (RING, 0, UP, 3, 5), (RING, 0, DOWN, 3, 2), (RING, 0, UP, 3, 0),
-    (RING, 0, DOWN, 3, 3), (RING, 0, UP, 3, 1), (RING, 0, DOWN, 3, 4), (RING, 0, UP, 3, 2),
-    (RING, 0, DOWN, 3, 5), (TERM, 1, 0), (RING, 1, UP, 0, 0), (TERM, 1, 3), (RING, 1, DOWN, 0, 3),
-    (TERM, 1, 1), (RING, 1, UP, 0, 1), (TERM, 1, 4), (RING, 1, DOWN, 0, 4), (TERM, 1, 2),
-    (RING, 1, UP, 0, 2), (TERM, 1, 5), (RING, 1, DOWN, 0, 5), (RING, 1, UP, 1, 3),
-    (RING, 1, DOWN, 1, 0), (RING, 1, UP, 1, 4), (RING, 1, DOWN, 1, 1), (RING, 1, UP, 1, 5),
-    (RING, 1, DOWN, 1, 2), (LAST, 0, 0), (LAST, 0, 3), (LAST, 0, 1), (LAST, 0, 4), (LAST, 0, 2),
-    (LAST, 0, 5), (RING, 1, UP, 1, 0), (RING, 1, DOWN, 1, 3), (RING, 1, UP, 1, 1),
-    (RING, 1, DOWN, 1, 4), (RING, 1, UP, 1, 2), (RING, 1, DOWN, 1, 5), (RING, 1, UP, 2, 3),
-    (RING, 1, DOWN, 2, 0), (RING, 1, UP, 2, 4), (RING, 1, DOWN, 2, 1), (RING, 1, UP, 2, 5),
-    (RING, 1, DOWN, 2, 2), (RING, 1, UP, 2, 0), (RING, 1, DOWN, 2, 3), (RING, 1, UP, 2, 1),
-    (RING, 1, DOWN, 2, 4), (RING, 1, UP, 2, 2), (RING, 1, DOWN, 2, 5), (RING, 1, UP, 3, 3),
-    (RING, 1, DOWN, 3, 0), (RING, 1, UP, 3, 4), (RING, 1, DOWN, 3, 1), (RING, 1, UP, 3, 5),
-    (RING, 1, DOWN, 3, 2), (RING, 1, UP, 3, 0), (RING, 1, DOWN, 3, 3), (RING, 1, UP, 3, 1),
-    (RING, 1, DOWN, 3, 4), (RING, 1, UP, 3, 2), (RING, 1, DOWN, 3, 5), (LAST, 1, 0), (LAST, 1, 3),
-    (LAST, 1, 1), (LAST, 1, 4), (LAST, 1, 2), (LAST, 1, 5), (FINISH,),
+    (OWN_Y, CACHE, 0), (TOKENS, 0, DOWN, 1, 0), (OWN_X, CACHE, 0), (TOKENS, 0, UP, 1, 0),
+    (FROM_Y, QKV, 1, 0), (TOKENS, 0, UP, 1, 1), (FROM_Y, QKV, 1, 1), (FROM_X, QKV, DOWN, 0, 1),
+    (READY,), (OWN_X, OUT, 0), (FROM_X, QKV, UP, 1, 0), (FROM_X, CACHE, DOWN, 0, 0),
+    (FIRST_OWN_X, CACHE), (TOKENS, 0, UP, 2, 1), (FROM_X, QKV, DOWN, 1, 0), (OWN_X, OUT, 1),
+    (TOKENS, 0, DOWN, 1, 1), (FROM_Y, CACHE, 1, 0), (FROM_X, CACHE, UP, 0, 0),
+    (FROM_X, QKV, UP, 0, 0), (FIRST_OWN_Y, CACHE), (FROM_X, QKV, UP, 0, 1), (TOKENS, 0, DOWN, 2, 0),
+    (FROM_Y, QKV, 2, 1), (FROM_X, QKV, DOWN, 1, 1), (TOKENS_OWN, 1), (FROM_Y, QKV, 2, 0),
+    (TOKENS, 0, DOWN, 2, 1), (FROM_Y, QKV, 3, 0), (OWN_Y, OUT, 1), (TOKENS, 1, UP, 1, 0),
+    (TOKENS, 0, UP, 2, 0), (FROM_Y, QKV, 3, 1), (TOKENS, 1, DOWN, 1, 1),
+    (FIRST_FROM_Y, CACHE, 0, 1), (FROM_Y, CACHE, 3, 0), (FROM_X, QKV, DOWN, 2, 1),
+    (TOKENS, 1, UP, 1, 1), (FROM_OPPOSITE, QKV, DOWN, 0), (OWN_Y, OUT, 0), (FROM_X, OUT, UP, 0, 1),
+    (FIRST_FROM_X, CACHE, DOWN), (FIRST_FROM_X, CACHE, UP), (FROM_OPPOSITE, QKV, UP, 0),
+    (TOKENS, 1, DOWN, 1, 0), (TOKENS, 0, DOWN, 3, 1), (FROM_X, QKV, UP, 2, 0),
+    (TOKENS, 1, UP, 2, 0), (FROM_X, QKV, UP, 2, 1), (TOKENS, 1, DOWN, 2, 1), (FROM_Y, OUT, 1, 1),
+    (FIRST_FROM_Y, CACHE, 0, 2), (FIRST_FROM_Y, CACHE, 0, 3), (FROM_X, QKV, DOWN, 0, 0),
+    (TOKENS, 0, UP, 3, 0), (FROM_X, QKV, UP, 3, 0), (TOKENS, 1, DOWN, 2, 0),
+    (FROM_X, QKV, DOWN, 3, 1), (FROM_OPPOSITE, QKV, UP, 1), (FROM_Y, CACHE, 2, 0),
+    (FROM_X, QKV, UP, 1, 1), (TOKENS, 0, DOWN, 4, 1), (TOKENS, 1, UP, 2, 1), (FROM_Y, OUT, 2, 1),
+    (FROM_Y, OUT, 2, 0), (ARRIVED, QKV, 0), (FROM_OPPOSITE, QKV, DOWN, 2), (TOKENS, 1, UP, 3, 0),
+    (FROM_Y, OUT, 1, 0), (FROM_X, QKV, DOWN, 2, 0), (FROM_Y, OUT, 3, 1), (TOKENS, 1, DOWN, 3, 1),
+    (FROM_X, QKV, UP, 3, 1), (FIRST_FROM_Y, CACHE, -1, 1), (TOKENS, 0, DOWN, 3, 0),
+    (FROM_X, OUT, DOWN, 0, 0), (FROM_X, QKV, DOWN, 3, 0), (FIRST_FROM_Y, CACHE, 1, 1),
+    (FIRST_FROM_OPPOSITE, CACHE), (FROM_X, OUT, DOWN, 0, 1), (FROM_X, OUT, UP, 1, 1),
+    (FROM_OPPOSITE, QKV, UP, 3), (FROM_X, CACHE, UP, 1, 0), (FROM_X, OUT, DOWN, 1, 1),
+    (FROM_OPPOSITE, QKV, DOWN, 1), (FROM_X, CACHE, DOWN, 1, 0), (TOKENS, 0, UP, 4, 0),
+    (FROM_Y, OUT, 3, 0), (FROM_OPPOSITE, QKV, UP, 2), (FROM_X, OUT, UP, 0, 0),
+    (FROM_X, CACHE, UP, 3, 0), (TOKENS, 1, UP, 3, 1), (FROM_OPPOSITE, QKV, DOWN, 3),
+    (TOKENS, 0, UP, 3, 1), (TOKENS, 1, DOWN, 3, 0), (FIRST_FROM_Y, CACHE, -1, 2), (ARRIVED, QKV, 1),
+    (FROM_X, CACHE, DOWN, 3, 0), (ARRIVED, QKV, -1), (ARRIVED, QKV, 2), (TOKENS, 1, UP, 4, 0),
+    (TOKENS, 1, DOWN, 4, 1), (PROJECT,), (SEGMENT, 0), (FROM_X, OUT, UP, 1, 0),
+    (FIRST_FROM_Y, CACHE, -1, 3), (FROM_X, CACHE, UP, 2, 0), (FIRST_FROM_Y, CACHE, 2, 1),
+    (FROM_X, OUT, DOWN, 3, 1), (FIRST_FROM_Y, CACHE, 1, 2), (FROM_X, OUT, UP, 2, 0),
+    (ARRIVED, CACHE, 0), (ATTEND, 0, 0), (FROM_X, OUT, UP, 3, 1), (FIRST_FROM_Y, CACHE, 1, 3),
+    (FROM_X, OUT, DOWN, 2, 1), (FROM_X, CACHE, DOWN, 2, 0), (FROM_X, OUT, DOWN, 2, 0),
+    (FROM_OPPOSITE, CACHE, UP, 1), (FROM_X, OUT, DOWN, 1, 0), (ARRIVED, CACHE, -1),
+    (FROM_X, OUT, UP, 3, 0), (FROM_X, OUT, DOWN, 3, 0), (FIRST_FROM_Y, CACHE, 2, 2),
+    (ATTEND, 0, -1), (FROM_OPPOSITE, CACHE, UP, 0), (FIRST_FROM_Y, CACHE, 2, 3),
+    (FROM_OPPOSITE, CACHE, UP, 3), (ARRIVED, CACHE, 1), (FROM_OPPOSITE, CACHE, UP, 2),
+    (ATTEND, 0, 1), (FROM_X, OUT, UP, 2, 1), (ARRIVED, CACHE, 2), (ATTEND, 0, 2), (ARRIVED, OUT, 0),
+    (ARRIVED, OUT, -1), (ARRIVED, OUT, 1), (CLOSE, 0), (TERM, 0, 0), (SWAP,), (TERM, 0, 1),
+    (RING, 0, UP, 0, 1), (RING, 0, DOWN, 1, 1), (TERM, 0, 2), (RING, 0, UP, 0, 2),
+    (RING, 0, DOWN, 1, 2), (TERM, 0, 3), (RING, 0, DOWN, 0, 3), (RING, 0, UP, 1, 3),
+    (FROM_OPPOSITE, OUT, DOWN, 0), (FROM_OPPOSITE, OUT, UP, 1), (FROM_OPPOSITE, OUT, UP, 0),
+    (FROM_OPPOSITE, OUT, DOWN, 3), (FROM_OPPOSITE, OUT, DOWN, 1), (FROM_OPPOSITE, OUT, DOWN, 2),
+    (FROM_OPPOSITE, OUT, UP, 2), (FROM_OPPOSITE, OUT, UP, 3), (ARRIVED, OUT, 2), (TERM, 0, 4),
+    (RING, 0, DOWN, 0, 4), (RING, 0, UP, 1, 4), (TERM, 0, 5), (RING, 0, DOWN, 0, 5),
+    (RING, 0, UP, 1, 5), (SEGMENT, 1), (ATTEND, 1, 0), (RING, 0, UP, 1, 1), (RING, 0, DOWN, 1, 3),
+    (RING, 0, UP, 1, 2), (RING, 0, DOWN, 1, 4), (RING, 0, DOWN, 1, 5), (ATTEND, 1, -1),
+    (ATTEND, 1, 1), (RING, 0, UP, 2, 3), (RING, 0, DOWN, 2, 1), (RING, 0, UP, 2, 4),
+    (RING, 0, DOWN, 2, 2), (RING, 0, UP, 2, 5), (RING, 0, DOWN, 2, 3), (RING, 0, UP, 2, 1),
+    (RING, 0, DOWN, 2, 4), (RING, 0, UP, 2, 2), (RING, 0, DOWN, 2, 5), (ATTEND, 1, 2), (CLOSE, 1),
+    (RING, 0, UP, 3, 3), (RING, 0, DOWN, 3, 1), (RING, 0, UP, 3, 4), (RING, 0, DOWN, 3, 2),
+    (RING, 0, UP, 3, 5), (RING, 0, DOWN, 3, 3), (RING, 0, UP, 3, 1), (RING, 0, DOWN, 3, 4),
+    (RING, 0, UP, 3, 2), (RING, 0, DOWN, 3, 5), (TERM, 1, 1), (RING, 1, UP, 0, 1), (TERM, 1, 3),
+    (RING, 1, DOWN, 0, 3), (TERM, 1, 2), (RING, 1, UP, 0, 2), (TERM, 1, 4), (RING, 1, DOWN, 0, 4),
+    (TERM, 1, 5), (RING, 1, DOWN, 0, 5), (RING, 1, UP, 1, 3), (RING, 1, DOWN, 1, 1),
+    (RING, 1, UP, 1, 4), (RING, 1, DOWN, 1, 2), (RING, 1, UP, 1, 5), (TERM, 1, 0), (ADD,),
+    (RING, 1, UP, 0, 0), (RING, 1, DOWN, 1, 0), (RING, 1, UP, 1, 1), (RING, 1, DOWN, 1, 3),
+    (RING, 1, UP, 1, 2), (RING, 1, DOWN, 1, 4), (RING, 1, DOWN, 1, 5), (LAST, 0, 1), (LAST, 0, 3),
+    (LAST, 0, 2), (LAST, 0, 4), (LAST, 0, 5), (RING, 1, UP, 1, 0), (RING, 1, UP, 2, 3),
+    (RING, 1, DOWN, 2, 1), (RING, 1, UP, 2, 4), (RING, 1, DOWN, 2, 2), (RING, 1, UP, 2, 5),
+    (RING, 1, DOWN, 2, 0), (RING, 1, UP, 2, 1), (RING, 1, DOWN, 2, 3), (RING, 1, UP, 2, 2),
+    (RING, 1, DOWN, 2, 4), (RING, 1, UP, 2, 0), (RING, 1, DOWN, 2, 5), (RING, 1, UP, 3, 3),
+    (RING, 1, DOWN, 3, 1), (RING, 1, UP, 3, 4), (RING, 1, DOWN, 3, 2), (RING, 1, UP, 3, 5),
+    (RING, 1, DOWN, 3, 0), (RING, 1, UP, 3, 1), (RING, 1, DOWN, 3, 3), (RING, 1, UP, 3, 2),
+    (RING, 1, DOWN, 3, 4), (RING, 1, UP, 3, 0), (RING, 1, DOWN, 3, 5), (LAST, 1, 3), (LAST, 1, 1),
+    (LAST, 1, 4), (LAST, 1, 2), (LAST, 1, 5), (LAST, 1, 0), (FINISH,),
 )
 
 def rope_rows(positions, head_dim):
@@ -126,7 +125,7 @@
     table, length_ref, tool,
     out,
     hid, ing, og, qg, kg, wo, ck, tables,
-    tok, wb, kvb, wob, wsrc, wst, osrc, ost, term, ru, rd, ysend, yrecv, total,
+    tok, wb, kvb, wob, wsrc, wst, osrc, ost, term, ru, rd, ysend, yrecv, zbuf, total,
     proj, queries, seg_keys, seg_values, attended, att_acc, row_best, row_total,
     load_sems, send_sems, recv_sems,
 ):
@@ -264,6 +263,9 @@
             self.steps = {
                 OWN_Y: self.own_y, OWN_X: self.own_x, FROM_Y: self.y_step,
                 FROM_X: self.x_step, FROM_OPPOSITE: self.o_step, ARRIVED: self.arrived,
+                FIRST_OWN_X: self.first_own_x, FIRST_OWN_Y: self.first_own_y,
+                FIRST_FROM_X: self.first_from_x, FIRST_FROM_OPPOSITE: self.first_from_opposite,
+                FIRST_FROM_Y: self.first_from_y,
             }
 
         def at(self, dx, i, k, core=c):
@@ -314,6 +316,52 @@
             recv((self.name, "o", way, i), block)
             send((self.name, "s", 2, i, k), block, sibling)
 
+
+        def first_y(self, dx):
+            block = self.at(dx, 0, 1)
+            send((self.name, "fyn", dx), block, y_next)
+            send((self.name, "fym", dx, 0), block, y_middle, when=inner == 1)
+
+        def first_own_x(self):
+            block = self.at(0, 0, 1)
+            send((self.name, "f", UP), block, x_up)
+            send((self.name, "f", DOWN), block, x_down)
+            send((self.name, "s", 0, 0, 1), block, sibling)
+
+        def first_own_y(self):
+            self.first_y(0)
+
+        def first_from_x(self, way):
+            dx, where = (-1, x_up) if way == UP else (1, x_down)
+            block = self.at(dx, 0, 1)
+            recv((self.name, "f", way), block)
+            send((self.name, "fo", way), self.at(dx, 0, 2 + way), where)
+            self.first_y(dx)
+            send((self.name, "s", dx, 0, 1), block, sibling)
+
+        def first_from_opposite(self):
+            recv((self.name, "fo", UP), self.at(2, 0, 2 + UP))
+            recv((self.name, "fo", DOWN), self.at(2, 0, 2 + DOWN))
+            self.first_y(2)
+            send((self.name, "s", 2, 0, 1), self.at(2, 0, 1), sibling)
+
+        def first_from_y(self, dx, i):
+            block = self.at(dx, i, 1)
+            if i == 1:
+                recv((self.name, "fyn", dx), block)
+                send((self.name, "fym", dx, 1), block, y_middle, when=inner == 1)
+            else:
+                @pl.when(inner == 1)
+                def _():
+                    recv((self.name, "fym", dx, i - 2), block)
+
+                @pl.when(inner == 0)
+                def _():
+                    recv((self.name, "fye", dx, i), block)
+
+                send((self.name, "fye", dx, i), block, y_end, when=inner == 1)
+            send((self.name, "s", dx, i, 1), block, sibling)
+
         def arrived(self, dx):
             for i in range(NY):
                 for k in range(2):
@@ -330,8 +378,8 @@
         start, size = cache_parts[k]
         return kvb.at[pl.ds(pl.multiple_of((chip * NC + core) * block_rows + start, 16), size)]
 
-    pair_parts = ((0, 176), (176, 160))
-    cache_parts = ((0, 80), (80, 80))
+    pair_parts = ((0, 176), (176, 160), (176, 80), (256, 80))
+    cache_parts = ((0, 80), (80, 80), (80, 48), (128, 32))
     gathers = {
         QKV: Gather("W", pair_rows(wb)),
         CACHE: Gather("C", cache_rows),
@@ -444,16 +492,23 @@
         for half in range(2):
             attended[g, :, half * hd : (half + 1) * hd] = combined[half * rows : (half + 1) * rows]
 
+    x_half, x_odd = lax.div(x, 2), lax.rem(x, 2)
+
+    def columns_of(p):
+        near = x_half if p < 3 else 1 - x_half
+        place = p + x_odd * (2 - 2 * p) if p < 3 else (5 - p) + x_odd * (2 * p - 8)
+        return pl.ds(pl.multiple_of((near * 3 + place) * piece, 128), piece)
+
     def term_at(g, dz, p):
         return (
             pl.ds(
                 pl.multiple_of((group_y[g] * NZ + wrap(z + dz, NZ)) * own_rows, own_rows), own_rows
             ),
-            pl.ds(p * piece, piece),
+            columns_of(p),
         )
 
     def make_term(g, p):
-        at = pl.ds(p * piece, piece)
+        at = columns_of(p)
         columns = jnp.concatenate([wob[0, at, :], wob[1, at, :]], axis=1)
         place = pl.ds(pl.multiple_of(group_y[g] * rows, rows), rows)
         term[place, at] = nt_dot(attended[g], columns).astype(BF16)
@@ -466,6 +521,15 @@
             recv(("R", g, way, k - 1, p), buf.at[g, k - 1, p])
             term[at] = (term[at].astype(F32) + buf[g, k - 1, p].astype(F32)).astype(BF16)
         send(("R", g, way, k, p), term.at[at], where, buf.at[g, k, p])
+
+    def swap_terms():
+        place = pl.ds(pl.multiple_of(group_y[0] * rows, rows), rows)
+        send(("Z",), term.at[place, columns_of(0)], partner, zbuf)
+
+    def add_swapped():
+        recv(("Z",), zbuf)
+        at = (pl.ds(pl.multiple_of(group_y[1] * rows, rows), rows), columns_of(0))
+        term[at] = (term[at].astype(F32) + zbuf[...].astype(F32)).astype(BF16)
 
     def ring_last(g, p):
         recv(("R", g, UP, 3, p), ru.at[g, 3, p])
@@ -478,9 +542,11 @@
         if g == 0:
             ysend[p] = summed.astype(BF16)
             send(("Y", p), ysend.at[p], partner, yrecv.at[p])
+        elif p == 0:
+            total[:, columns_of(p)] = summed
         else:
             recv(("Y", p), yrecv.at[p])
-            total[:, p * piece : (p + 1) * piece] = summed + yrecv[p].astype(F32)
+            total[:, columns_of(p)] = summed + yrecv[p].astype(F32)
 
     def finish():
         loaded("og")
@@ -499,7 +565,7 @@
     steps = {
         TOKENS: token_step, TOKENS_OWN: token_own, READY: own_out_ready, PROJECT: project_all,
         SEGMENT: attend_segment, ATTEND: attend_group, CLOSE: close_group,
-        TERM: make_term, RING: ring_step, LAST: ring_last, FINISH: finish,
+        TERM: make_term, RING: ring_step, SWAP: swap_terms, ADD: add_swapped, LAST: ring_last, FINISH: finish,
     }
 
     for op, *what in ORDER:
@@ -570,6 +636,7 @@
             pltpu.VMEM((2, 4, PIECES, own_rows, piece), BF16),
             pltpu.VMEM((PIECES, own_rows, piece), BF16),
             pltpu.VMEM((PIECES, own_rows, piece), BF16),
+            pltpu.VMEM((seg // NH, piece), BF16),
             pltpu.VMEM((own_rows, width), F32),
             pltpu.VMEM((seg, 4 * hd), F32),
             pltpu.VMEM((NH, seg, hd), BF16),

time: 108 us -> 103 us (0.954)
  Pallas kernels: 105 us -> 101 us
    pallas_call x1, Pallas kernels: 105 us -> 101 us  [on_device(): pl.pallas_call(kernel, out_shape=jax.ShapeDtypeStruct((own_rows, width),...]
where the time goes in v3:
time: 103 us
  Pallas kernels  101 us (98%)
  local copies, waits for them, and re-layouts  1.6 us (2%)
    pallas_call x1, Pallas kernels, on_device(): pl.pallas_call(kernel, out_shape=jax.ShapeDtypeStruct((own_rows, width),...  101 us

profile of v3, /device:TPU:1, one launch (start us, length us, event | category | flops | bytes accessed | tf_op | source)
XLA Modules:
  0.0 102.9 jit_solution(3113930013902294315)
XLA Ops:
  0.7 100.7 %shard_map.145 = bf16[16,5376]{1,0:T(8,128)(2,1)} custom-call(bf16[16,5376]{1,0:T(8,128)(2,1)} %bitcast.6, f32[5376]{0:T(1024)} %ing_in.1, bf16[168,256]{1,0:T(8,128)(2,1)} %wq_in.1, bf16[168,128]{1,0:T(8,128)(2,1)} %wk_in.1, bf16[168,128]{1,0:T(8,128)(2,1)} %wv_in.1, f32[1,128]{1,0:T(1,128)} %bitcast.8, f32[1,128]{1,0:T(1,128)} %bitcast.9, ...), custom_call_target="tpu_custom_call" | custom-call | tf_op jit(solution)/shard_map/pallas_call | solution.py:612
  101.3 1.6 %copy.18 = bf16[1,16,5376]{2,1,0:T(8,128)(2,1)} copy(bf16[1,16,5376]{2,1,0:T(8,128)(2,1)} %bitcast.5) | data formatting | bytes 344064

commit v4 on v3

--- a/solution.py
+++ b/solution.py
@@ -19,80 +19,81 @@
 PIECES = 6
 
 (
-    TOKENS, TOKENS_OWN, READY, PROJECT, SEGMENT, ATTEND, CLOSE, TERM, RING, SWAP, ADD, LAST, FINISH,
+    TOKENS, TOKENS_SWAP, TOKENS_OWN, READY, PROJECT, SEGMENT, ATTEND, CLOSE, TERM, RING, SWAP, ADD, LAST, FINISH,
     OWN_Y, OWN_X, FROM_Y, FROM_X, FROM_OPPOSITE, ARRIVED,
     FIRST_OWN_X, FIRST_OWN_Y, FIRST_FROM_X, FIRST_FROM_OPPOSITE, FIRST_FROM_Y,
-) = range(24)
+) = range(25)
 UP, DOWN = range(2)
 QKV, CACHE, OUT = range(3)
 ORDER = (
-    (OWN_Y, CACHE, 0), (TOKENS, 0, DOWN, 1, 0), (OWN_X, CACHE, 0), (TOKENS, 0, UP, 1, 0),
-    (FROM_Y, QKV, 1, 0), (TOKENS, 0, UP, 1, 1), (FROM_Y, QKV, 1, 1), (FROM_X, QKV, DOWN, 0, 1),
-    (READY,), (OWN_X, OUT, 0), (FROM_X, QKV, UP, 1, 0), (FROM_X, CACHE, DOWN, 0, 0),
-    (FIRST_OWN_X, CACHE), (TOKENS, 0, UP, 2, 1), (FROM_X, QKV, DOWN, 1, 0), (OWN_X, OUT, 1),
-    (TOKENS, 0, DOWN, 1, 1), (FROM_Y, CACHE, 1, 0), (FROM_X, CACHE, UP, 0, 0),
-    (FROM_X, QKV, UP, 0, 0), (FIRST_OWN_Y, CACHE), (FROM_X, QKV, UP, 0, 1), (TOKENS, 0, DOWN, 2, 0),
-    (FROM_Y, QKV, 2, 1), (FROM_X, QKV, DOWN, 1, 1), (TOKENS_OWN, 1), (FROM_Y, QKV, 2, 0),
-    (TOKENS, 0, DOWN, 2, 1), (FROM_Y, QKV, 3, 0), (OWN_Y, OUT, 1), (TOKENS, 1, UP, 1, 0),
-    (TOKENS, 0, UP, 2, 0), (FROM_Y, QKV, 3, 1), (TOKENS, 1, DOWN, 1, 1),
-    (FIRST_FROM_Y, CACHE, 0, 1), (FROM_Y, CACHE, 3, 0), (FROM_X, QKV, DOWN, 2, 1),
-    (TOKENS, 1, UP, 1, 1), (FROM_OPPOSITE, QKV, DOWN, 0), (OWN_Y, OUT, 0), (FROM_X, OUT, UP, 0, 1),
-    (FIRST_FROM_X, CACHE, DOWN), (FIRST_FROM_X, CACHE, UP), (FROM_OPPOSITE, QKV, UP, 0),
-    (TOKENS, 1, DOWN, 1, 0), (TOKENS, 0, DOWN, 3, 1), (FROM_X, QKV, UP, 2, 0),
-    (TOKENS, 1, UP, 2, 0), (FROM_X, QKV, UP, 2, 1), (TOKENS, 1, DOWN, 2, 1), (FROM_Y, OUT, 1, 1),
-    (FIRST_FROM_Y, CACHE, 0, 2), (FIRST_FROM_Y, CACHE, 0, 3), (FROM_X, QKV, DOWN, 0, 0),
-    (TOKENS, 0, UP, 3, 0), (FROM_X, QKV, UP, 3, 0), (TOKENS, 1, DOWN, 2, 0),
-    (FROM_X, QKV, DOWN, 3, 1), (FROM_OPPOSITE, QKV, UP, 1), (FROM_Y, CACHE, 2, 0),
-    (FROM_X, QKV, UP, 1, 1), (TOKENS, 0, DOWN, 4, 1), (TOKENS, 1, UP, 2, 1), (FROM_Y, OUT, 2, 1),
-    (FROM_Y, OUT, 2, 0), (ARRIVED, QKV, 0), (FROM_OPPOSITE, QKV, DOWN, 2), (TOKENS, 1, UP, 3, 0),
-    (FROM_Y, OUT, 1, 0), (FROM_X, QKV, DOWN, 2, 0), (FROM_Y, OUT, 3, 1), (TOKENS, 1, DOWN, 3, 1),
-    (FROM_X, QKV, UP, 3, 1), (FIRST_FROM_Y, CACHE, -1, 1), (TOKENS, 0, DOWN, 3, 0),
-    (FROM_X, OUT, DOWN, 0, 0), (FROM_X, QKV, DOWN, 3, 0), (FIRST_FROM_Y, CACHE, 1, 1),
-    (FIRST_FROM_OPPOSITE, CACHE), (FROM_X, OUT, DOWN, 0, 1), (FROM_X, OUT, UP, 1, 1),
-    (FROM_OPPOSITE, QKV, UP, 3), (FROM_X, CACHE, UP, 1, 0), (FROM_X, OUT, DOWN, 1, 1),
-    (FROM_OPPOSITE, QKV, DOWN, 1), (FROM_X, CACHE, DOWN, 1, 0), (TOKENS, 0, UP, 4, 0),
-    (FROM_Y, OUT, 3, 0), (FROM_OPPOSITE, QKV, UP, 2), (FROM_X, OUT, UP, 0, 0),
-    (FROM_X, CACHE, UP, 3, 0), (TOKENS, 1, UP, 3, 1), (FROM_OPPOSITE, QKV, DOWN, 3),
-    (TOKENS, 0, UP, 3, 1), (TOKENS, 1, DOWN, 3, 0), (FIRST_FROM_Y, CACHE, -1, 2), (ARRIVED, QKV, 1),
-    (FROM_X, CACHE, DOWN, 3, 0), (ARRIVED, QKV, -1), (ARRIVED, QKV, 2), (TOKENS, 1, UP, 4, 0),
-    (TOKENS, 1, DOWN, 4, 1), (PROJECT,), (SEGMENT, 0), (FROM_X, OUT, UP, 1, 0),
-    (FIRST_FROM_Y, CACHE, -1, 3), (FROM_X, CACHE, UP, 2, 0), (FIRST_FROM_Y, CACHE, 2, 1),
-    (FROM_X, OUT, DOWN, 3, 1), (FIRST_FROM_Y, CACHE, 1, 2), (FROM_X, OUT, UP, 2, 0),
-    (ARRIVED, CACHE, 0), (ATTEND, 0, 0), (FROM_X, OUT, UP, 3, 1), (FIRST_FROM_Y, CACHE, 1, 3),
-    (FROM_X, OUT, DOWN, 2, 1), (FROM_X, CACHE, DOWN, 2, 0), (FROM_X, OUT, DOWN, 2, 0),
-    (FROM_OPPOSITE, CACHE, UP, 1), (FROM_X, OUT, DOWN, 1, 0), (ARRIVED, CACHE, -1),
-    (FROM_X, OUT, UP, 3, 0), (FROM_X, OUT, DOWN, 3, 0), (FIRST_FROM_Y, CACHE, 2, 2),
-    (ATTEND, 0, -1), (FROM_OPPOSITE, CACHE, UP, 0), (FIRST_FROM_Y, CACHE, 2, 3),
-    (FROM_OPPOSITE, CACHE, UP, 3), (ARRIVED, CACHE, 1), (FROM_OPPOSITE, CACHE, UP, 2),
-    (ATTEND, 0, 1), (FROM_X, OUT, UP, 2, 1), (ARRIVED, CACHE, 2), (ATTEND, 0, 2), (ARRIVED, OUT, 0),
-    (ARRIVED, OUT, -1), (ARRIVED, OUT, 1), (CLOSE, 0), (TERM, 0, 0), (SWAP,), (TERM, 0, 1),
-    (RING, 0, UP, 0, 1), (RING, 0, DOWN, 1, 1), (TERM, 0, 2), (RING, 0, UP, 0, 2),
-    (RING, 0, DOWN, 1, 2), (TERM, 0, 3), (RING, 0, DOWN, 0, 3), (RING, 0, UP, 1, 3),
-    (FROM_OPPOSITE, OUT, DOWN, 0), (FROM_OPPOSITE, OUT, UP, 1), (FROM_OPPOSITE, OUT, UP, 0),
-    (FROM_OPPOSITE, OUT, DOWN, 3), (FROM_OPPOSITE, OUT, DOWN, 1), (FROM_OPPOSITE, OUT, DOWN, 2),
-    (FROM_OPPOSITE, OUT, UP, 2), (FROM_OPPOSITE, OUT, UP, 3), (ARRIVED, OUT, 2), (TERM, 0, 4),
-    (RING, 0, DOWN, 0, 4), (RING, 0, UP, 1, 4), (TERM, 0, 5), (RING, 0, DOWN, 0, 5),
-    (RING, 0, UP, 1, 5), (SEGMENT, 1), (ATTEND, 1, 0), (RING, 0, UP, 1, 1), (RING, 0, DOWN, 1, 3),
-    (RING, 0, UP, 1, 2), (RING, 0, DOWN, 1, 4), (RING, 0, DOWN, 1, 5), (ATTEND, 1, -1),
-    (ATTEND, 1, 1), (RING, 0, UP, 2, 3), (RING, 0, DOWN, 2, 1), (RING, 0, UP, 2, 4),
-    (RING, 0, DOWN, 2, 2), (RING, 0, UP, 2, 5), (RING, 0, DOWN, 2, 3), (RING, 0, UP, 2, 1),
-    (RING, 0, DOWN, 2, 4), (RING, 0, UP, 2, 2), (RING, 0, DOWN, 2, 5), (ATTEND, 1, 2), (CLOSE, 1),
-    (RING, 0, UP, 3, 3), (RING, 0, DOWN, 3, 1), (RING, 0, UP, 3, 4), (RING, 0, DOWN, 3, 2),
-    (RING, 0, UP, 3, 5), (RING, 0, DOWN, 3, 3), (RING, 0, UP, 3, 1), (RING, 0, DOWN, 3, 4),
-    (RING, 0, UP, 3, 2), (RING, 0, DOWN, 3, 5), (TERM, 1, 1), (RING, 1, UP, 0, 1), (TERM, 1, 3),
-    (RING, 1, DOWN, 0, 3), (TERM, 1, 2), (RING, 1, UP, 0, 2), (TERM, 1, 4), (RING, 1, DOWN, 0, 4),
-    (TERM, 1, 5), (RING, 1, DOWN, 0, 5), (RING, 1, UP, 1, 3), (RING, 1, DOWN, 1, 1),
-    (RING, 1, UP, 1, 4), (RING, 1, DOWN, 1, 2), (RING, 1, UP, 1, 5), (TERM, 1, 0), (ADD,),
-    (RING, 1, UP, 0, 0), (RING, 1, DOWN, 1, 0), (RING, 1, UP, 1, 1), (RING, 1, DOWN, 1, 3),
-    (RING, 1, UP, 1, 2), (RING, 1, DOWN, 1, 4), (RING, 1, DOWN, 1, 5), (LAST, 0, 1), (LAST, 0, 3),
-    (LAST, 0, 2), (LAST, 0, 4), (LAST, 0, 5), (RING, 1, UP, 1, 0), (RING, 1, UP, 2, 3),
-    (RING, 1, DOWN, 2, 1), (RING, 1, UP, 2, 4), (RING, 1, DOWN, 2, 2), (RING, 1, UP, 2, 5),
-    (RING, 1, DOWN, 2, 0), (RING, 1, UP, 2, 1), (RING, 1, DOWN, 2, 3), (RING, 1, UP, 2, 2),
-    (RING, 1, DOWN, 2, 4), (RING, 1, UP, 2, 0), (RING, 1, DOWN, 2, 5), (RING, 1, UP, 3, 3),
-    (RING, 1, DOWN, 3, 1), (RING, 1, UP, 3, 4), (RING, 1, DOWN, 3, 2), (RING, 1, UP, 3, 5),
-    (RING, 1, DOWN, 3, 0), (RING, 1, UP, 3, 1), (RING, 1, DOWN, 3, 3), (RING, 1, UP, 3, 2),
-    (RING, 1, DOWN, 3, 4), (RING, 1, UP, 3, 0), (RING, 1, DOWN, 3, 5), (LAST, 1, 3), (LAST, 1, 1),
-    (LAST, 1, 4), (LAST, 1, 2), (LAST, 1, 5), (LAST, 1, 0), (FINISH,),
+    (READY,), (OWN_X, OUT, 0), (OWN_Y, CACHE, 0), (TOKENS, 0, UP, 1, 0), (TOKENS_SWAP, 0),
+    (TOKENS, 0, DOWN, 1, 1), (OWN_X, CACHE, 0), (TOKENS_SWAP, 1), (FROM_Y, QKV, 1, 0),
+    (OWN_X, OUT, 1), (TOKENS, 0, UP, 1, 1), (TOKENS, 0, DOWN, 1, 0), (FROM_X, CACHE, UP, 0, 0),
+    (FROM_X, OUT, DOWN, 0, 0), (FROM_X, QKV, UP, 0, 0), (FIRST_OWN_X, CACHE), (FROM_Y, QKV, 1, 1),
+    (FROM_Y, CACHE, 1, 0), (TOKENS, 0, DOWN, 2, 1), (TOKENS, 0, DOWN, 2, 0),
+    (FROM_X, QKV, UP, 1, 0), (TOKENS_OWN, 0), (FIRST_OWN_Y, CACHE), (TOKENS, 0, UP, 2, 0),
+    (FROM_X, QKV, DOWN, 0, 1), (FROM_Y, QKV, 2, 0), (TOKENS_OWN, 1), (FROM_Y, QKV, 2, 1),
+    (FIRST_FROM_Y, CACHE, 0, 1), (OWN_Y, OUT, 1), (FROM_X, CACHE, DOWN, 0, 0),
+    (FROM_X, QKV, DOWN, 1, 1), (TOKENS, 0, DOWN, 3, 1), (TOKENS, 1, UP, 1, 0),
+    (FROM_X, OUT, UP, 0, 1), (FROM_Y, QKV, 3, 0), (TOKENS, 0, UP, 2, 1), (TOKENS, 1, DOWN, 1, 0),
+    (FROM_Y, QKV, 3, 1), (OWN_Y, OUT, 0), (TOKENS, 1, DOWN, 1, 1), (TOKENS, 1, UP, 1, 1),
+    (FROM_Y, CACHE, 3, 0), (FROM_X, QKV, UP, 0, 1), (FROM_OPPOSITE, QKV, DOWN, 0),
+    (TOKENS, 1, UP, 2, 0), (FROM_X, QKV, DOWN, 1, 0), (FIRST_FROM_X, CACHE, UP),
+    (FROM_X, QKV, UP, 2, 0), (FIRST_FROM_X, CACHE, DOWN), (FROM_X, QKV, UP, 2, 1),
+    (FROM_X, QKV, DOWN, 2, 1), (TOKENS, 0, UP, 3, 0), (FROM_OPPOSITE, QKV, DOWN, 1),
+    (FROM_Y, OUT, 1, 1), (FROM_X, QKV, DOWN, 3, 0), (FROM_X, QKV, DOWN, 2, 0),
+    (TOKENS, 1, DOWN, 2, 1), (FROM_OPPOSITE, CACHE, UP, 0), (FROM_OPPOSITE, QKV, UP, 1),
+    (FIRST_FROM_Y, CACHE, 0, 3), (TOKENS, 1, DOWN, 2, 0), (FROM_X, QKV, UP, 3, 0),
+    (FROM_X, QKV, DOWN, 0, 0), (TOKENS, 0, DOWN, 4, 1), (FROM_Y, CACHE, 2, 0),
+    (FROM_X, QKV, DOWN, 3, 1), (FROM_X, QKV, UP, 1, 1), (TOKENS, 1, UP, 2, 1), (ARRIVED, QKV, 0),
+    (FROM_Y, OUT, 2, 1), (FROM_OPPOSITE, QKV, UP, 0), (FROM_Y, OUT, 1, 0),
+    (FIRST_FROM_OPPOSITE, CACHE), (TOKENS, 1, UP, 3, 0), (FROM_Y, OUT, 3, 1),
+    (TOKENS, 1, DOWN, 3, 1), (FROM_X, CACHE, UP, 3, 0), (FROM_OPPOSITE, QKV, DOWN, 2),
+    (ARRIVED, QKV, 1), (FROM_X, QKV, UP, 3, 1), (FROM_Y, OUT, 2, 0), (FROM_Y, OUT, 3, 0),
+    (TOKENS, 1, UP, 3, 1), (FIRST_FROM_Y, CACHE, 0, 2), (FROM_OPPOSITE, QKV, UP, 2),
+    (FIRST_FROM_Y, CACHE, -1, 1), (FROM_X, CACHE, DOWN, 1, 0), (FROM_X, OUT, DOWN, 0, 1),
+    (ARRIVED, QKV, -1), (FIRST_FROM_Y, CACHE, -1, 2), (FROM_X, CACHE, DOWN, 3, 0),
+    (FROM_X, OUT, DOWN, 1, 1), (FROM_X, CACHE, UP, 1, 0), (TOKENS, 0, DOWN, 3, 0),
+    (TOKENS, 1, UP, 4, 0), (FROM_X, CACHE, DOWN, 2, 0), (TOKENS, 0, UP, 3, 1),
+    (FROM_OPPOSITE, QKV, DOWN, 3), (FIRST_FROM_Y, CACHE, 1, 1), (FROM_OPPOSITE, QKV, UP, 3),
+    (TOKENS, 1, DOWN, 4, 1), (FIRST_FROM_Y, CACHE, 2, 2), (TOKENS, 1, DOWN, 3, 0),
+    (ARRIVED, OUT, 0), (FROM_X, OUT, UP, 1, 1), (TOKENS, 0, UP, 4, 0), (FROM_X, CACHE, UP, 2, 0),
+    (FROM_X, OUT, UP, 0, 0), (FROM_X, OUT, DOWN, 2, 1), (FIRST_FROM_Y, CACHE, 2, 1),
+    (ARRIVED, QKV, 2), (FIRST_FROM_Y, CACHE, -1, 3), (PROJECT,), (SEGMENT, 0),
+    (FIRST_FROM_Y, CACHE, 1, 3), (ARRIVED, CACHE, 0), (ATTEND, 0, 0), (FROM_X, OUT, DOWN, 3, 0),
+    (FROM_X, OUT, UP, 1, 0), (FROM_X, OUT, DOWN, 2, 0), (FIRST_FROM_Y, CACHE, 1, 2),
+    (FROM_X, OUT, DOWN, 3, 1), (FROM_X, OUT, DOWN, 1, 0), (ARRIVED, CACHE, -1),
+    (FROM_X, OUT, UP, 3, 1), (FROM_X, OUT, UP, 2, 0), (ATTEND, 0, -1), (FIRST_FROM_Y, CACHE, 2, 3),
+    (FROM_OPPOSITE, CACHE, UP, 1), (FROM_X, OUT, UP, 2, 1), (FROM_OPPOSITE, CACHE, UP, 3),
+    (FROM_X, OUT, UP, 3, 0), (FROM_OPPOSITE, CACHE, UP, 2), (ARRIVED, CACHE, 1), (ARRIVED, OUT, 1),
+    (ATTEND, 0, 1), (ARRIVED, OUT, -1), (ARRIVED, CACHE, 2), (ATTEND, 0, 2), (CLOSE, 0),
+    (TERM, 0, 0), (SWAP,), (TERM, 0, 1), (RING, 0, UP, 0, 1), (RING, 0, DOWN, 1, 1), (TERM, 0, 2),
+    (RING, 0, UP, 0, 2), (RING, 0, DOWN, 1, 2), (TERM, 0, 3), (RING, 0, DOWN, 0, 3),
+    (RING, 0, UP, 1, 3), (FROM_OPPOSITE, OUT, UP, 1), (FROM_OPPOSITE, OUT, DOWN, 0),
+    (FROM_OPPOSITE, OUT, DOWN, 1), (FROM_OPPOSITE, OUT, UP, 2), (FROM_OPPOSITE, OUT, UP, 3),
+    (FROM_OPPOSITE, OUT, UP, 0), (FROM_OPPOSITE, OUT, DOWN, 2), (FROM_OPPOSITE, OUT, DOWN, 3),
+    (ARRIVED, OUT, 2), (TERM, 0, 4), (RING, 0, DOWN, 0, 4), (RING, 0, UP, 1, 4), (TERM, 0, 5),
+    (RING, 0, DOWN, 0, 5), (RING, 0, UP, 1, 5), (SEGMENT, 1), (ATTEND, 1, 0), (RING, 0, UP, 1, 1),
+    (RING, 0, DOWN, 1, 3), (RING, 0, UP, 1, 2), (RING, 0, DOWN, 1, 4), (RING, 0, DOWN, 1, 5),
+    (ATTEND, 1, -1), (ATTEND, 1, 1), (RING, 0, UP, 2, 3), (RING, 0, DOWN, 2, 1),
+    (RING, 0, UP, 2, 4), (RING, 0, DOWN, 2, 2), (RING, 0, UP, 2, 5), (RING, 0, DOWN, 2, 3),
+    (RING, 0, UP, 2, 1), (RING, 0, DOWN, 2, 4), (RING, 0, UP, 2, 2), (RING, 0, DOWN, 2, 5),
+    (ATTEND, 1, 2), (CLOSE, 1), (RING, 0, UP, 3, 3), (RING, 0, DOWN, 3, 1), (RING, 0, UP, 3, 4),
+    (RING, 0, DOWN, 3, 2), (RING, 0, UP, 3, 5), (RING, 0, DOWN, 3, 3), (RING, 0, UP, 3, 1),
+    (RING, 0, DOWN, 3, 4), (RING, 0, UP, 3, 2), (RING, 0, DOWN, 3, 5), (TERM, 1, 1),
+    (RING, 1, UP, 0, 1), (TERM, 1, 3), (RING, 1, DOWN, 0, 3), (TERM, 1, 2), (RING, 1, UP, 0, 2),
+    (TERM, 1, 4), (RING, 1, DOWN, 0, 4), (TERM, 1, 5), (RING, 1, DOWN, 0, 5), (RING, 1, UP, 1, 3),
+    (RING, 1, DOWN, 1, 1), (RING, 1, UP, 1, 4), (RING, 1, DOWN, 1, 2), (RING, 1, UP, 1, 5),
+    (TERM, 1, 0), (ADD,), (RING, 1, UP, 0, 0), (RING, 1, DOWN, 1, 0), (RING, 1, UP, 1, 1),
+    (RING, 1, DOWN, 1, 3), (RING, 1, UP, 1, 2), (RING, 1, DOWN, 1, 4), (RING, 1, DOWN, 1, 5),
+    (LAST, 0, 1), (LAST, 0, 3), (LAST, 0, 2), (LAST, 0, 4), (LAST, 0, 5), (RING, 1, UP, 1, 0),
+    (RING, 1, UP, 2, 3), (RING, 1, DOWN, 2, 1), (RING, 1, UP, 2, 4), (RING, 1, DOWN, 2, 2),
+    (RING, 1, UP, 2, 5), (RING, 1, DOWN, 2, 0), (RING, 1, UP, 2, 1), (RING, 1, DOWN, 2, 3),
+    (RING, 1, UP, 2, 2), (RING, 1, DOWN, 2, 4), (RING, 1, UP, 2, 0), (RING, 1, DOWN, 2, 5),
+    (RING, 1, UP, 3, 3), (RING, 1, DOWN, 3, 1), (RING, 1, UP, 3, 4), (RING, 1, DOWN, 3, 2),
+    (RING, 1, UP, 3, 5), (RING, 1, DOWN, 3, 0), (RING, 1, UP, 3, 1), (RING, 1, DOWN, 3, 3),
+    (RING, 1, UP, 3, 2), (RING, 1, DOWN, 3, 4), (RING, 1, UP, 3, 0), (RING, 1, DOWN, 3, 5),
+    (LAST, 1, 3), (LAST, 1, 1), (LAST, 1, 4), (LAST, 1, 2), (LAST, 1, 5), (LAST, 1, 0), (FINISH,),
 )
 
 def rope_rows(positions, head_dim):
@@ -234,14 +235,14 @@
     def token_key(group, way, distance, part):
         return ("T", group, way, distance, part)
 
-    def token_own(group):
-        yy = yh if group == 0 else 1 - yh
-        for part in range(2):
-            if group == 1:
-                recv(("TP", part), token_block(z, yy, part))
-            block = token_block(z, yy, part)
-            send(token_key(group, UP, 1, part), block, z_up)
-            send(token_key(group, DOWN, 1, part), block, z_down)
+    def token_send(group, part):
+        block = token_block(z, yh if group == 0 else 1 - yh, part)
+        send(token_key(group, UP, 1, part), block, z_up)
+        send(token_key(group, DOWN, 1, part), block, z_down)
+
+    def token_own(part):
+        recv(("TP", part), token_block(z, 1 - yh, part))
+        token_send(1, part)
 
     def token_step(group, way, distance, part):
         yy = yh if group == 0 else 1 - yh
@@ -251,11 +252,11 @@
         if distance < 3 or (distance == 3 and part == last):
             send(token_key(group, way, distance + 1, part), block, where)
 
-    def token_partner():
-        for part in range(2):
-            send(("TP", part), token_block(z, yh, part), partner)
-
-    token_own(0)
+    def token_partner(part):
+        send(("TP", part), token_block(z, yh, part), partner)
+
+    token_send(0, 0)
+    token_send(0, 1)
 
     class Gather:
         def __init__(self, name, rows):
@@ -398,7 +399,6 @@
     for k in range(2):
         gathers[QKV].own_y(k)
         gathers[QKV].own_x(k)
-    token_partner()
 
     slot_block = table[roll]
     loaded("tables", "ck")
@@ -563,7 +563,7 @@
         wob[c, pl.ds(pl.multiple_of(chip * pair, 16), pair), :] = join_pair(osrc[c], ost[...])
 
     steps = {
-        TOKENS: token_step, TOKENS_OWN: token_own, READY: own_out_ready, PROJECT: project_all,
+        TOKENS: token_step, TOKENS_SWAP: token_partner, TOKENS_OWN: token_own, READY: own_out_ready, PROJECT: project_all,
         SEGMENT: attend_segment, ATTEND: attend_group, CLOSE: close_group,
         TERM: make_term, RING: ring_step, SWAP: swap_terms, ADD: add_swapped, LAST: ring_last, FINISH: finish,
     }

time: 103 us -> 101 us (0.981)
  Pallas kernels: 101 us -> 98.4 us
    pallas_call x1, Pallas kernels: 101 us -> 98.4 us  [on_device(): pl.pallas_call(kernel, out_shape=jax.ShapeDtypeStruct((own_rows, width),...]
where the time goes in v4:
time: 101 us
  Pallas kernels  98.4 us (97%)
  local copies, waits for them, and re-layouts  1.6 us (2%)
    pallas_call x1, Pallas kernels, on_device(): pl.pallas_call(kernel, out_shape=jax.ShapeDtypeStruct((own_rows, width),...  98.4 us

profile of v4, /device:TPU:1, one launch (start us, length us, event | category | flops | bytes accessed | tf_op | source)
XLA Modules:
  0.0 100.7 jit_solution(6676977596996483253)
XLA Ops:
  0.7 98.4 %shard_map.145 = bf16[16,5376]{1,0:T(8,128)(2,1)} custom-call(bf16[16,5376]{1,0:T(8,128)(2,1)} %bitcast.6, f32[5376]{0:T(1024)} %ing_in.1, bf16[168,256]{1,0:T(8,128)(2,1)} %wq_in.1, bf16[168,128]{1,0:T(8,128)(2,1)} %wk_in.1, bf16[168,128]{1,0:T(8,128)(2,1)} %wv_in.1, f32[1,128]{1,0:T(1,128)} %bitcast.8, f32[1,128]{1,0:T(1,128)} %bitcast.9, ...), custom_call_target="tpu_custom_call" | custom-call | tf_op jit(solution)/shard_map/pallas_call | solution.py:612
  99.1 1.6 %copy.18 = bf16[1,16,5376]{2,1,0:T(8,128)(2,1)} copy(bf16[1,16,5376]{2,1,0:T(8,128)(2,1)} %bitcast.5) | data formatting | bytes 344064

commit v5 on v4

--- a/solution.py
+++ b/solution.py
@@ -26,52 +26,52 @@
 UP, DOWN = range(2)
 QKV, CACHE, OUT = range(3)
 ORDER = (
-    (READY,), (OWN_X, OUT, 0), (OWN_Y, CACHE, 0), (TOKENS, 0, UP, 1, 0), (TOKENS_SWAP, 0),
-    (TOKENS, 0, DOWN, 1, 1), (OWN_X, CACHE, 0), (TOKENS_SWAP, 1), (FROM_Y, QKV, 1, 0),
-    (OWN_X, OUT, 1), (TOKENS, 0, UP, 1, 1), (TOKENS, 0, DOWN, 1, 0), (FROM_X, CACHE, UP, 0, 0),
-    (FROM_X, OUT, DOWN, 0, 0), (FROM_X, QKV, UP, 0, 0), (FIRST_OWN_X, CACHE), (FROM_Y, QKV, 1, 1),
-    (FROM_Y, CACHE, 1, 0), (TOKENS, 0, DOWN, 2, 1), (TOKENS, 0, DOWN, 2, 0),
-    (FROM_X, QKV, UP, 1, 0), (TOKENS_OWN, 0), (FIRST_OWN_Y, CACHE), (TOKENS, 0, UP, 2, 0),
-    (FROM_X, QKV, DOWN, 0, 1), (FROM_Y, QKV, 2, 0), (TOKENS_OWN, 1), (FROM_Y, QKV, 2, 1),
-    (FIRST_FROM_Y, CACHE, 0, 1), (OWN_Y, OUT, 1), (FROM_X, CACHE, DOWN, 0, 0),
-    (FROM_X, QKV, DOWN, 1, 1), (TOKENS, 0, DOWN, 3, 1), (TOKENS, 1, UP, 1, 0),
-    (FROM_X, OUT, UP, 0, 1), (FROM_Y, QKV, 3, 0), (TOKENS, 0, UP, 2, 1), (TOKENS, 1, DOWN, 1, 0),
-    (FROM_Y, QKV, 3, 1), (OWN_Y, OUT, 0), (TOKENS, 1, DOWN, 1, 1), (TOKENS, 1, UP, 1, 1),
-    (FROM_Y, CACHE, 3, 0), (FROM_X, QKV, UP, 0, 1), (FROM_OPPOSITE, QKV, DOWN, 0),
-    (TOKENS, 1, UP, 2, 0), (FROM_X, QKV, DOWN, 1, 0), (FIRST_FROM_X, CACHE, UP),
-    (FROM_X, QKV, UP, 2, 0), (FIRST_FROM_X, CACHE, DOWN), (FROM_X, QKV, UP, 2, 1),
-    (FROM_X, QKV, DOWN, 2, 1), (TOKENS, 0, UP, 3, 0), (FROM_OPPOSITE, QKV, DOWN, 1),
-    (FROM_Y, OUT, 1, 1), (FROM_X, QKV, DOWN, 3, 0), (FROM_X, QKV, DOWN, 2, 0),
-    (TOKENS, 1, DOWN, 2, 1), (FROM_OPPOSITE, CACHE, UP, 0), (FROM_OPPOSITE, QKV, UP, 1),
-    (FIRST_FROM_Y, CACHE, 0, 3), (TOKENS, 1, DOWN, 2, 0), (FROM_X, QKV, UP, 3, 0),
-    (FROM_X, QKV, DOWN, 0, 0), (TOKENS, 0, DOWN, 4, 1), (FROM_Y, CACHE, 2, 0),
-    (FROM_X, QKV, DOWN, 3, 1), (FROM_X, QKV, UP, 1, 1), (TOKENS, 1, UP, 2, 1), (ARRIVED, QKV, 0),
-    (FROM_Y, OUT, 2, 1), (FROM_OPPOSITE, QKV, UP, 0), (FROM_Y, OUT, 1, 0),
-    (FIRST_FROM_OPPOSITE, CACHE), (TOKENS, 1, UP, 3, 0), (FROM_Y, OUT, 3, 1),
-    (TOKENS, 1, DOWN, 3, 1), (FROM_X, CACHE, UP, 3, 0), (FROM_OPPOSITE, QKV, DOWN, 2),
-    (ARRIVED, QKV, 1), (FROM_X, QKV, UP, 3, 1), (FROM_Y, OUT, 2, 0), (FROM_Y, OUT, 3, 0),
-    (TOKENS, 1, UP, 3, 1), (FIRST_FROM_Y, CACHE, 0, 2), (FROM_OPPOSITE, QKV, UP, 2),
-    (FIRST_FROM_Y, CACHE, -1, 1), (FROM_X, CACHE, DOWN, 1, 0), (FROM_X, OUT, DOWN, 0, 1),
-    (ARRIVED, QKV, -1), (FIRST_FROM_Y, CACHE, -1, 2), (FROM_X, CACHE, DOWN, 3, 0),
-    (FROM_X, OUT, DOWN, 1, 1), (FROM_X, CACHE, UP, 1, 0), (TOKENS, 0, DOWN, 3, 0),
-    (TOKENS, 1, UP, 4, 0), (FROM_X, CACHE, DOWN, 2, 0), (TOKENS, 0, UP, 3, 1),
-    (FROM_OPPOSITE, QKV, DOWN, 3), (FIRST_FROM_Y, CACHE, 1, 1), (FROM_OPPOSITE, QKV, UP, 3),
-    (TOKENS, 1, DOWN, 4, 1), (FIRST_FROM_Y, CACHE, 2, 2), (TOKENS, 1, DOWN, 3, 0),
-    (ARRIVED, OUT, 0), (FROM_X, OUT, UP, 1, 1), (TOKENS, 0, UP, 4, 0), (FROM_X, CACHE, UP, 2, 0),
-    (FROM_X, OUT, UP, 0, 0), (FROM_X, OUT, DOWN, 2, 1), (FIRST_FROM_Y, CACHE, 2, 1),
-    (ARRIVED, QKV, 2), (FIRST_FROM_Y, CACHE, -1, 3), (PROJECT,), (SEGMENT, 0),
-    (FIRST_FROM_Y, CACHE, 1, 3), (ARRIVED, CACHE, 0), (ATTEND, 0, 0), (FROM_X, OUT, DOWN, 3, 0),
-    (FROM_X, OUT, UP, 1, 0), (FROM_X, OUT, DOWN, 2, 0), (FIRST_FROM_Y, CACHE, 1, 2),
-    (FROM_X, OUT, DOWN, 3, 1), (FROM_X, OUT, DOWN, 1, 0), (ARRIVED, CACHE, -1),
-    (FROM_X, OUT, UP, 3, 1), (FROM_X, OUT, UP, 2, 0), (ATTEND, 0, -1), (FIRST_FROM_Y, CACHE, 2, 3),
-    (FROM_OPPOSITE, CACHE, UP, 1), (FROM_X, OUT, UP, 2, 1), (FROM_OPPOSITE, CACHE, UP, 3),
-    (FROM_X, OUT, UP, 3, 0), (FROM_OPPOSITE, CACHE, UP, 2), (ARRIVED, CACHE, 1), (ARRIVED, OUT, 1),
-    (ATTEND, 0, 1), (ARRIVED, OUT, -1), (ARRIVED, CACHE, 2), (ATTEND, 0, 2), (CLOSE, 0),
-    (TERM, 0, 0), (SWAP,), (TERM, 0, 1), (RING, 0, UP, 0, 1), (RING, 0, DOWN, 1, 1), (TERM, 0, 2),
-    (RING, 0, UP, 0, 2), (RING, 0, DOWN, 1, 2), (TERM, 0, 3), (RING, 0, DOWN, 0, 3),
-    (RING, 0, UP, 1, 3), (FROM_OPPOSITE, OUT, UP, 1), (FROM_OPPOSITE, OUT, DOWN, 0),
-    (FROM_OPPOSITE, OUT, DOWN, 1), (FROM_OPPOSITE, OUT, UP, 2), (FROM_OPPOSITE, OUT, UP, 3),
-    (FROM_OPPOSITE, OUT, UP, 0), (FROM_OPPOSITE, OUT, DOWN, 2), (FROM_OPPOSITE, OUT, DOWN, 3),
+    (READY,), (OWN_X, OUT, 0), (OWN_Y, CACHE, 0), (OWN_X, OUT, 1), (OWN_X, CACHE, 0),
+    (TOKENS_SWAP, 0), (TOKENS, 0, DOWN, 1, 1), (TOKENS, 0, UP, 1, 0), (TOKENS_SWAP, 1),
+    (TOKENS, 0, UP, 1, 1), (FROM_Y, QKV, 1, 0), (FROM_Y, QKV, 1, 1), (TOKENS, 0, DOWN, 1, 0),
+    (OWN_Y, OUT, 1), (FROM_Y, CACHE, 1, 0), (TOKENS, 0, UP, 2, 0), (FROM_X, QKV, UP, 0, 0),
+    (FROM_X, QKV, UP, 1, 0), (FIRST_OWN_X, CACHE), (FROM_X, CACHE, UP, 0, 0),
+    (TOKENS, 0, DOWN, 2, 1), (FIRST_OWN_Y, CACHE), (FROM_X, QKV, DOWN, 1, 0), (TOKENS_OWN, 0),
+    (TOKENS, 0, UP, 2, 1), (FROM_X, QKV, DOWN, 0, 1), (FROM_X, CACHE, DOWN, 1, 0),
+    (FROM_X, QKV, DOWN, 1, 1), (FROM_Y, QKV, 2, 1), (TOKENS, 0, DOWN, 2, 0), (TOKENS_OWN, 1),
+    (FROM_Y, QKV, 2, 0), (FROM_X, QKV, UP, 0, 1), (FROM_X, QKV, DOWN, 0, 0),
+    (TOKENS, 1, DOWN, 1, 0), (TOKENS, 1, UP, 1, 0), (FROM_Y, QKV, 3, 0), (FROM_Y, QKV, 3, 1),
+    (FIRST_FROM_Y, CACHE, 0, 1), (TOKENS, 1, UP, 1, 1), (OWN_Y, OUT, 0), (TOKENS, 1, DOWN, 1, 1),
+    (FROM_Y, CACHE, 3, 0), (TOKENS, 0, DOWN, 3, 1), (FIRST_FROM_X, CACHE, DOWN),
+    (TOKENS, 0, UP, 3, 0), (FIRST_FROM_X, CACHE, UP), (FROM_X, QKV, DOWN, 2, 0),
+    (TOKENS, 1, UP, 2, 0), (FROM_Y, OUT, 1, 1), (FROM_X, QKV, DOWN, 2, 1), (FROM_X, OUT, UP, 0, 1),
+    (FROM_OPPOSITE, QKV, UP, 1), (FROM_X, QKV, UP, 3, 0), (FROM_X, QKV, UP, 2, 0),
+    (FROM_Y, CACHE, 2, 0), (TOKENS, 1, DOWN, 2, 1), (FROM_X, QKV, DOWN, 3, 1),
+    (FROM_X, OUT, DOWN, 0, 1), (FIRST_FROM_Y, CACHE, 0, 3), (FROM_X, QKV, UP, 1, 1),
+    (FROM_X, QKV, UP, 2, 1), (FROM_X, QKV, UP, 3, 1), (FROM_OPPOSITE, QKV, UP, 0),
+    (TOKENS, 1, DOWN, 2, 0), (TOKENS, 1, UP, 2, 1), (FROM_X, CACHE, DOWN, 3, 0),
+    (FROM_Y, OUT, 2, 0), (FROM_X, OUT, DOWN, 0, 0), (TOKENS, 0, DOWN, 3, 0), (FROM_Y, OUT, 2, 1),
+    (FROM_Y, OUT, 1, 0), (FROM_X, QKV, DOWN, 3, 0), (FIRST_FROM_OPPOSITE, CACHE),
+    (TOKENS, 1, UP, 3, 0), (FIRST_FROM_Y, CACHE, 1, 1), (FROM_OPPOSITE, QKV, DOWN, 0),
+    (TOKENS, 1, DOWN, 3, 1), (FROM_Y, OUT, 3, 1), (FROM_Y, OUT, 3, 0), (FIRST_FROM_Y, CACHE, 0, 2),
+    (ARRIVED, QKV, 0), (TOKENS, 0, UP, 3, 1), (FROM_X, CACHE, UP, 1, 0), (FROM_X, OUT, UP, 0, 0),
+    (FROM_OPPOSITE, QKV, DOWN, 2), (TOKENS, 0, DOWN, 4, 1), (ARRIVED, OUT, 0),
+    (FROM_OPPOSITE, CACHE, UP, 0), (FROM_X, CACHE, UP, 3, 0), (TOKENS, 1, UP, 3, 1),
+    (FROM_OPPOSITE, QKV, UP, 3), (FROM_OPPOSITE, QKV, DOWN, 1), (FIRST_FROM_Y, CACHE, -1, 2),
+    (TOKENS, 1, DOWN, 3, 0), (FROM_X, CACHE, DOWN, 0, 0), (FROM_X, CACHE, DOWN, 2, 0),
+    (FROM_OPPOSITE, QKV, UP, 2), (FROM_X, OUT, DOWN, 1, 1), (ARRIVED, QKV, 1),
+    (FROM_OPPOSITE, QKV, DOWN, 3), (FIRST_FROM_Y, CACHE, 2, 2), (FROM_X, OUT, UP, 1, 1),
+    (FIRST_FROM_Y, CACHE, -1, 1), (ARRIVED, QKV, -1), (TOKENS, 0, UP, 4, 0),
+    (TOKENS, 1, DOWN, 4, 1), (FROM_X, CACHE, UP, 2, 0), (TOKENS, 1, UP, 4, 0), (ARRIVED, QKV, 2),
+    (PROJECT,), (SEGMENT, 0), (FIRST_FROM_Y, CACHE, 2, 1), (FROM_X, OUT, UP, 2, 1),
+    (FIRST_FROM_Y, CACHE, 1, 3), (ARRIVED, CACHE, 0), (FIRST_FROM_Y, CACHE, -1, 3),
+    (FROM_X, OUT, UP, 3, 1), (ATTEND, 0, 0), (FROM_X, OUT, DOWN, 2, 1), (FROM_X, OUT, UP, 1, 0),
+    (ARRIVED, CACHE, -1), (FROM_X, OUT, DOWN, 3, 1), (FROM_X, OUT, UP, 3, 0),
+    (FIRST_FROM_Y, CACHE, 1, 2), (FROM_X, OUT, DOWN, 2, 0), (FROM_X, OUT, DOWN, 1, 0),
+    (FROM_OPPOSITE, OUT, DOWN, 0), (FROM_X, OUT, UP, 2, 0), (FROM_X, OUT, DOWN, 3, 0),
+    (ATTEND, 0, -1), (FROM_OPPOSITE, CACHE, UP, 1), (FIRST_FROM_Y, CACHE, 2, 3),
+    (FROM_OPPOSITE, CACHE, UP, 3), (ARRIVED, OUT, -1), (ARRIVED, CACHE, 1),
+    (FROM_OPPOSITE, CACHE, UP, 2), (ATTEND, 0, 1), (ARRIVED, OUT, 1), (FROM_OPPOSITE, OUT, UP, 0),
+    (ARRIVED, CACHE, 2), (ATTEND, 0, 2), (CLOSE, 0), (TERM, 0, 0), (SWAP,), (TERM, 0, 1),
+    (RING, 0, UP, 0, 1), (RING, 0, DOWN, 1, 1), (TERM, 0, 2), (RING, 0, UP, 0, 2),
+    (RING, 0, DOWN, 1, 2), (TERM, 0, 3), (RING, 0, DOWN, 0, 3), (RING, 0, UP, 1, 3),
+    (FROM_OPPOSITE, OUT, UP, 3), (FROM_OPPOSITE, OUT, DOWN, 2), (FROM_OPPOSITE, OUT, DOWN, 1),
+    (FROM_OPPOSITE, OUT, UP, 1), (FROM_OPPOSITE, OUT, UP, 2), (FROM_OPPOSITE, OUT, DOWN, 3),
     (ARRIVED, OUT, 2), (TERM, 0, 4), (RING, 0, DOWN, 0, 4), (RING, 0, UP, 1, 4), (TERM, 0, 5),
     (RING, 0, DOWN, 0, 5), (RING, 0, UP, 1, 5), (SEGMENT, 1), (ATTEND, 1, 0), (RING, 0, UP, 1, 1),
     (RING, 0, DOWN, 1, 3), (RING, 0, UP, 1, 2), (RING, 0, DOWN, 1, 4), (RING, 0, DOWN, 1, 5),

time: 101 us -> 101 us (level)
  no operation moved by 1% of the time
where the time goes in v5:
time: 101 us; the launch traced here: 100 us
  Pallas kernels  98.2 us (97%)
  local copies, waits for them, and re-layouts  1.6 us (2%)
    pallas_call x1, Pallas kernels, on_device(): pl.pallas_call(kernel, out_shape=jax.ShapeDtypeStruct((own_rows, width),...  98.2 us

profile of v5, /device:TPU:1, one launch (start us, length us, event | category | flops | bytes accessed | tf_op | source)
XLA Modules:
  0.0 100.5 jit_solution(16778080559278778804)
XLA Ops:
  0.7 98.2 %shard_map.145 = bf16[16,5376]{1,0:T(8,128)(2,1)} custom-call(bf16[16,5376]{1,0:T(8,128)(2,1)} %bitcast.6, f32[5376]{0:T(1024)} %ing_in.1, bf16[168,256]{1,0:T(8,128)(2,1)} %wq_in.1, bf16[168,128]{1,0:T(8,128)(2,1)} %wk_in.1, bf16[168,128]{1,0:T(8,128)(2,1)} %wv_in.1, f32[1,128]{1,0:T(1,128)} %bitcast.8, f32[1,128]{1,0:T(1,128)} %bitcast.9, ...), custom_call_target="tpu_custom_call" | custom-call | tf_op jit(solution)/shard_map/pallas_call | solution.py:612
  98.9 1.6 %copy.18 = bf16[1,16,5376]{2,1,0:T(8,128)(2,1)} copy(bf16[1,16,5376]{2,1,0:T(8,128)(2,1)} %bitcast.5) | data formatting | bytes 344064
